TPU v7x, 256 devices: a whole 4x4x8 slice. The times are simulated.
256 devices in a mesh: energy: 32 (over z_lo, y, core), matrix: 8 (over x, z_hi).
Axes of the slice: x: 4, y: 4, z: 8 (z_hi: 2, z_lo: 4; z = z_hi * 4 + z_lo), core: 2. Of those that a mesh axis runs over, the one named last changes fastest.
Arguments:
- lesser: float32 [2, 2, 256, 131072], P(None, None, 'energy', 'matrix'), may hold values from -6 to 6
- greater_t: float32 [2, 2, 256, 131072], P(None, None, 'energy', 'matrix'), may hold values from -6 to 6
- panel_store: float32 [32, 256, 256], P('matrix'), may hold values from -0.1875 to 0.1875
- owner: int32 [4], replicated, may hold values from 0 to 7
- pattern: int32 [128, 4], P('matrix'), may hold values from 0 to 3, each once within a row
Outputs:
- polarization: float32 [2, 2, 256, 131072], P(None, None, 'energy', 'matrix')
- screened: float32 [2, 2, 256, 32768], P(None, None, 'energy', 'matrix')
Inputs may be any that keep to these rules, and one draw needn't show every extreme that they name: Panel b is stored in slot b of device owner[b] along matrix. Each row of pattern names every block once.
All inputs are finite; a program needn't handle non-finite values.
Results may differ from a plain program's by a relative error of at most 0.000098.
Values sent between devices are 32-bit elements; how exact they have to be, the bound alone decides.
No kernel may reach another device: no remote copies, remote signals or barrier semaphores. Data moves between devices by JAX's collectives and lax.ppermute only.
A program may use at most 64 MiB of HBM per device.

v0:
```python
import math

import jax
import jax.numpy as jnp
from jax import lax
from jax.sharding import PartitionSpec as P

NB = 4
NR = 256


def from_root(block, axis, holder):
    block = jnp.where(lax.axis_index(axis) == holder, block, jnp.zeros_like(block))
    return lax.psum(block, axis)


def apply_table(table, values):
    return jnp.einsum("ft,ktm->kfm", table, values, precision=lax.Precision.HIGHEST)


def apply_back(table, values):
    return jnp.einsum("ft,kfm->ktm", table, values, precision=lax.Precision.HIGHEST)


def local(lesser, greater_t, panel_store, owner, pattern):
    kpoints = lesser.shape[0]
    local_energy = lesser.shape[2]
    elements = lesser.shape[3]
    groups = lax.axis_size("energy")
    total_energy = local_energy * groups
    freq_count = 2 * total_energy
    energy_index = jnp.arange(total_energy, dtype=jnp.int32)
    freq_index = jnp.arange(freq_count, dtype=jnp.int32)
    phase_index = freq_index[:, None] * energy_index[None, :] % freq_count
    phase_angle = phase_index.astype(jnp.float32) * (2.0 * math.pi / freq_count)
    cosine_table = jnp.cos(phase_angle)
    sine_table = jnp.sin(phase_angle)
    prefactor = 1.0 / math.sqrt(total_energy)
    stacked = jnp.concatenate((lesser, greater_t), axis=1)
    stacked = stacked.reshape(kpoints * 4, local_energy, groups, elements // groups)
    pieces = lax.all_to_all(stacked, "energy", split_axis=2, concat_axis=1, tiled=True)
    count = pieces.shape[3]
    components = pieces.reshape(kpoints, 4, total_energy, count)
    left_re = components[:, 0]
    left_im = components[:, 1]
    right_re = components[:, 2]
    right_im = components[:, 3]
    fleft_re = apply_table(cosine_table, left_re) + apply_table(sine_table, left_im)
    fleft_im = apply_table(cosine_table, left_im) - apply_table(sine_table, left_re)
    fright_re = apply_table(cosine_table, right_re) - apply_table(sine_table, right_im)
    fright_im = apply_table(cosine_table, right_im) + apply_table(sine_table, right_re)
    joint_re = fleft_re * fright_re - fleft_im * fright_im
    joint_im = fleft_re * fright_im + fleft_im * fright_re
    correl_re = (apply_back(cosine_table, joint_re) - apply_back(sine_table, joint_im)) / freq_count
    correl_im = (apply_back(cosine_table, joint_im) + apply_back(sine_table, joint_re)) / freq_count
    result = jnp.stack((correl_im * prefactor, -correl_re * prefactor), axis=1)
    result = result.reshape(kpoints * 2, total_energy, 1, count)
    returned = lax.all_to_all(result, "energy", split_axis=1, concat_axis=2, tiled=True)
    polarization = returned.reshape(kpoints, 2, local_energy, elements)
    received = []
    for slot_index in range(NB):
        received.append(from_root(panel_store[slot_index], "matrix", owner[slot_index]))
    panels = jnp.stack(received)
    local_columns = elements // (NB * NR)
    shaped = polarization.reshape(kpoints, 2, local_energy, local_columns, NB, NR)
    chosen = jnp.take_along_axis(shaped, pattern[None, None, None, :, :, None], axis=4)
    screened = jnp.einsum("brs,kyecbs->kyecr", panels, chosen, precision=lax.Precision.HIGHEST)
    return (polarization, screened.reshape(kpoints, 2, local_energy, local_columns * NR))


def solution(mesh):
    in_specs = (
        P(None, None, "energy", "matrix"),
        P(None, None, "energy", "matrix"),
        P("matrix", None, None),
        P(),
        P("matrix", None),
    )
    out_specs = (P(None, None, "energy", "matrix"), P(None, None, "energy", "matrix"))
    return jax.shard_map(local, mesh=mesh, in_specs=in_specs, out_specs=out_specs, check_vma=False)
```

profile of v0, /device:TPU:8, one launch (start us, length us, event | category | flops | bytes accessed | tf_op | source)
XLA Modules:
  0.0 349.7 jit_solution(15915493552438055575)
XLA Ops:
  7.2 2.5 pad_maximum_fusion
  9.7 2.4 copy.54
  12.1 2.4 copy.30
  14.5 102.3 %all_to_all.30 = f32[8,8,32,512]{3,1,0,2:T(8,128)S(1)} all-to-all(f32[8,8,32,512]{3,1,0,2:T(8,128)S(1)} %copy.30), channel_id=1, replica_groups=mesh['energy'=32,'matrix'=8] {'energy'}, dimensions={2} | all-to-all | bytes 8388608 | tf_op jit(solution)/shard_map/all_to_all | solution.py:41
  117.5 5.2 %fusion.42 = f32[2,512,512]{2,1,0:T(8,128)S(1)} fusion(f32[2,4,256,512]{3,2,1,0:T(8,128)S(1)} %bitcast.135), kind=kOutput, calls=%fused_computation.43 | convolution fusion | flops 1612447744 | bytes 3145728 | tf_op jit(solution)/shard_map/ft,ktm->kfm/dot_general | solution.py:18
  122.6 5.2 %fusion.40 = f32[2,512,512]{2,1,0:T(8,128)S(1)} fusion(f32[2,4,256,512]{3,2,1,0:T(8,128)S(1)} %bitcast.136), kind=kOutput, calls=%fused_computation.41 | convolution fusion | flops 1612447744 | bytes 3145728 | tf_op jit(solution)/shard_map/ft,ktm->kfm/dot_general | solution.py:18
  127.8 5.3 %fusion.43 = f32[2,512,512]{2,1,0:T(8,128)S(1)} fusion(f32[2,4,256,512]{3,2,1,0:T(8,128)S(1)} %bitcast.137), kind=kOutput, calls=%fused_computation.44 | convolution fusion | flops 1612447744 | bytes 3145728 | tf_op jit(solution)/shard_map/ft,ktm->kfm/dot_general | solution.py:18
  133.1 5.1 %fusion.41 = f32[2,512,512]{2,1,0:T(8,128)S(1)} fusion(f32[2,4,256,512]{3,2,1,0:T(8,128)S(1)} %bitcast.138), kind=kOutput, calls=%fused_computation.42 | convolution fusion | flops 1612447744 | bytes 3145728 | tf_op jit(solution)/shard_map/ft,ktm->kfm/dot_general | solution.py:18
  138.3 5.4 %convolution_add_fusion = f32[2,512,512]{2,1,0:T(8,128)S(1)} fusion(f32[2,512,512]{2,1,0:T(8,128)S(1)} %fusion.42, f32[2,4,256,512]{3,2,1,0:T(8,128)S(1)} %bitcast.139), kind=kOutput, calls=%fused_computation.20 | convolution fusion | flops 1612972032 | bytes 5242880 | tf_op jit(solution)/shard_map/ft,ktm->kfm/dot_general | solution.py:18
  143.7 5.2 %convolution_add_fusion.1 = f32[2,512,512]{2,1,0:T(8,128)S(1)} fusion(f32[2,512,512]{2,1,0:T(8,128)S(1)} %fusion.40, f32[2,4,256,512]{3,2,1,0:T(8,128)S(1)} %bitcast.140), kind=kOutput, calls=%fused_computation.21 | convolution fusion | flops 1612972032 | bytes 5242880 | tf_op jit(solution)/shard_map/ft,ktm->kfm/dot_general | solution.py:18
  149.0 5.6 %convolution_subtract_fusion = f32[2,512,512]{2,1,0:T(8,128)S(1)} fusion(f32[2,512,512]{2,1,0:T(8,128)S(1)} %fusion.43, f32[2,4,256,512]{3,2,1,0:T(8,128)S(1)} %bitcast.141), kind=kOutput, calls=%fused_computation.18 | convolution fusion | flops 1612972032 | bytes 5242880 | tf_op jit(solution)/shard_map/ft,ktm->kfm/dot_general | solution.py:18
  154.5 5.5 %multiply_add_fusion = (f32[2,512,512]{2,1,0:T(8,128)S(1)}, f32[2,512,512]{2,1,0:T(8,128)S(1)}) fusion(f32[2,512,512]{2,1,0:T(8,128)S(1)} %convolution_subtract_fusion, f32[2,512,512]{2,1,0:T(8,128)S(1)} %convolution_add_fusion.1, f32[2,512,512]{2,1,0:T(8,128)S(1)} %convolution_add_fusion, f32[2,512,512]{2,1,0:T(8,128)S(1)} %fusion.41, ...), kind=kOutput, calls=%fused_computation.17 | convolution fusion | flops 1616117760 | bytes 13631488 | tf_op jit(solution)/shard_map/ft,ktm->kfm/dot_general | solution.py:18
  160.1 3.7 %fusion.2 = f32[2,512,256]{2,1,0:T(8,128)S(1)} fusion(f32[2,512,512]{2,1,0:T(8,128)S(1)} %get-tuple-element.7), kind=kOutput, calls=%fused_computation.6 | convolution fusion | flops 1612447744 | bytes 3145728 | tf_op jit(solution)/shard_map/ft,kfm->ktm/dot_general | solution.py:22
  163.8 3.9 %fusion = f32[2,512,256]{2,1,0:T(8,128)S(1)} fusion(f32[2,512,512]{2,1,0:T(8,128)S(1)} %get-tuple-element.7), kind=kOutput, calls=%fused_computation.4 | convolution fusion | flops 1612447744 | bytes 3145728 | tf_op jit(solution)/shard_map/ft,kfm->ktm/dot_general | solution.py:22
  167.7 3.7 %fusion.16 = f32[2,1,256,512]{2,3,0,1:T(8,128)S(1)} fusion(f32[2,512,256]{2,1,0:T(8,128)S(1)} %fusion.2, f32[2,512,512]{2,1,0:T(8,128)S(1)} %get-tuple-element.6), kind=kOutput, calls=%fused_computation.24 | convolution fusion | flops 1612972032 | bytes 4194304 | tf_op jit(solution)/shard_map/ft,kfm->ktm/dot_general | solution.py:22
  171.4 3.7 %fusion.31 = f32[2,1,256,512]{2,3,0,1:T(8,128)S(1)} fusion(f32[2,512,256]{2,1,0:T(8,128)S(1)} %fusion, f32[2,512,512]{2,1,0:T(8,128)S(1)} %get-tuple-element.6), kind=kOutput, calls=%fused_computation.29 | convolution fusion | flops 1613496320 | bytes 4194304 | tf_op jit(solution)/shard_map/ft,kfm->ktm/dot_general | solution.py:22
  177.3 4.3 %copy.37 = f32[4,256,1,512]{3,0,2,1:T(4,128)} copy(f32[4,256,1,512]{3,1,0,2:T(8,128)} %bitcast.147) | data formatting | bytes 4194304 | tf_op jit(solution)/shard_map/reshape | solution.py:57
  181.6 6.0 %all-to-all-start.1 = ((f32[4,256,1,512]{3,0,2,1:T(4,128)}), f32[4,256,1,512]{3,0,2,1:T(4,128)S(1)}, u32[]{:S(2)}, u32[]{:S(2)}) async-start(f32[4,256,1,512]{3,0,2,1:T(4,128)} %copy.37), calls=%async_computation.1 | async-start | bytes 4194304 | tf_op jit(solution)/shard_map/all_to_all | solution.py:58
  192.2 83.7 %all-to-all-done.1 = f32[4,256,1,512]{3,0,2,1:T(4,128)S(1)} async-done(((f32[4,256,1,512]{3,0,2,1:T(4,128)}), f32[4,256,1,512]{3,0,2,1:T(4,128)S(1)}, u32[]{:S(2)}, u32[]{:S(2)}) %all-to-all-start.1) | async-done | bytes 2097184 | tf_op jit(solution)/shard_map/all_to_all | solution.py:58
  277.2 2.8 copy.55
  283.6 2.8 copy.41
  286.4 2.0 gather_fusion
  288.4 49.8 %all-reduce.3.cloned.1.call-done = (f32[1,256,256]{2,1,0:T(8,128)}, f32[1,256,256]{2,1,0:T(8,128)}, f32[1,256,256]{2,1,0:T(8,128)}, f32[1,256,256]{2,1,0:T(8,128)}) async-done(((f32[1,256,256]{2,1,0:T(8,128)}, f32[1,256,256]{2,1,0:T(8,128)}, f32[1,256,256]{2,1,0:T(8,128)}, f32[1,256,256]{2,1,0:T(8,128)}), (f32[1,256,256]{2,1,0:T(8,128)}, f32[1,256,256]{2,1,0:T(8,128)}, f32[1,256,256]{2,1,0:T(8,128)}, ...) | async-done | bytes 1048592 | tf_op jit(solution)/shard_map/psum | solution.py:14
  338.2 4.5 %fusion.8 = f32[2,2,8,16,256,1]{4,2,5,3,1,0:T(8,128)} fusion(f32[1,256,256]{2,1,0:T(8,128)} %get-tuple-element.2, f32[1,256,256]{2,1,0:T(8,128)} %get-tuple-element.3, f32[1,256,256]{2,1,0:T(8,128)} %get-tuple-element.4, f32[1,256,256]{2,1,0:T(8,128)} %get-tuple-element.5, f32[16,4,2,2,8,256]{5,4,3,2,1,0:T(8,128)} %bitcast.148, pred[16,4]{1,0:T(8,128)(4,1)S(1)} %copy.39), kind=kOutput, calls=%fused_computation.12 | convolution fusion | flops 1611923456 | bytes 3670080 | tf_op jit(solution)/shard_map/brs,kyecbs->kyecr/dot_general | solution.py:67
  (22 shorter events, 9.6 us)
Async XLA Ops:
  181.6 6.1 %copy-start.3 = (s32[4]{0:T(128)S(1)}, s32[4]{0:T(128)}, u32[]{:S(2)}) copy-start(s32[4]{0:T(128)} %param.8) | copy-start | bytes 52
  181.6 9.3 %copy-start.1 = (f32[4,256,256]{2,1,0:T(8,128)S(1)}, f32[4,256,256]{2,1,0:T(8,128)}, u32[]{:S(2)}) copy-start(f32[4,256,256]{2,1,0:T(8,128)} %param.7) | copy-start | bytes 3145732
  181.6 94.3 %all-to-all-start.1 = ((f32[4,256,1,512]{3,0,2,1:T(4,128)}), f32[4,256,1,512]{3,0,2,1:T(4,128)S(1)}, u32[]{:S(2)}, u32[]{:S(2)}) async-start(f32[4,256,1,512]{3,0,2,1:T(4,128)} %copy.37), calls=%async_computation.1 | async-start | bytes 4194304 | tf_op jit(solution)/shard_map/all_to_all | solution.py:58
  187.6 4.3 %copy-start.2 = (s32[16,4]{0,1:T(4,128)S(1)}, s32[16,4]{0,1:T(4,128)}, u32[]{:S(2)}) copy-start(s32[16,4]{0,1:T(4,128)} %param.9) | copy-start | bytes 772
  187.6 150.6 %all-reduce.3.cloned.1.call-start = ((), (), s32[]{:S(2)}) async-start(), calls=%async_computation.2 | async-start | bytes 2097152 | tf_op jit(solution)/shard_map/psum | solution.py:14
  275.9 1.3 copy-start
Sparse Core Ops, SparseCore 0:
  192.0 146.1 all-reduce.2
where the time goes:
time: 355 us; the launch traced here: 350 us
  waiting for transfers between devices  133 us (37%)
  blocking collectives  102 us (29%)
  matrix products  62.1 us (17%)
  local copies, waits for them, and re-layouts  25.1 us (7%)
  between operations  17 us (5%)
  starting transfers between devices  6.06 us (2%)
  other arithmetic  3.67 us (1%)
    all_to_all x1, blocking collectives, local(): lax.all_to_all(stacked, 'energy', split_axis=2, concat_axis=1, tiled=True)  102 us
    all_to_all x1, waiting for transfers between devices, local(): lax.all_to_all(result, 'energy', split_axis=1, concat_axis=2, tiled=True)  83.7 us
    psum x1, waiting for transfers between devices, from_root(): return lax.psum(block, axis)  49.8 us
    dot_general x8, matrix products, apply_table(): jnp.einsum('ft,ktm->kfm', table, values, precision=lax.Precision.HIGHEST)  42.5 us
    dot_general x4, matrix products, apply_back(): jnp.einsum('ft,kfm->ktm', table, values, precision=lax.Precision.HIGHEST)  15.1 us
  transfers between devices with their start and end apart: 2, of which 2 were waited for; matrix products, arithmetic and copies ran while one was open for 4% of the time, Pallas kernels for 0%

commit v1 on v0

v1 whole, which is shorter than its diff:
```python
import functools
import math

import jax
import jax.numpy as jnp
import ml_dtypes
import numpy as np
from jax import lax
from jax.experimental import pallas as pl
from jax.experimental.pallas import tpu as pltpu
from jax.sharding import Mesh, PartitionSpec as P

NB = 4
NR = 256
F32 = jnp.float32
BF16 = jnp.bfloat16


def split_table(table):
    high = table.astype(ml_dtypes.bfloat16)
    low = (table - high.astype(np.float64)).astype(ml_dtypes.bfloat16)
    return np.stack((high, low))


def make_tables(block, scale):
    length = 2 * block
    freq = np.concatenate((np.arange(0, length, 2), np.arange(1, length, 2)))
    angle = (freq[:, None] * np.arange(block)[None, :] % length) * (2.0 * math.pi / length)
    cosine, sine = np.cos(angle), np.sin(angle)
    left = np.block([[cosine, sine], [-sine, cosine]])
    right = np.block([[cosine, -sine], [sine, cosine]])
    back = np.block([[sine.T, cosine.T], [-cosine.T, sine.T]]) * (scale / length)
    return split_table(left), split_table(right), split_table(back)


def split(values):
    high = values.astype(BF16)
    return high, (values - high.astype(F32)).astype(BF16)


def dot3(table, values):
    high, low = split(values)
    dot = functools.partial(jnp.dot, preferred_element_type=F32)
    return dot(table[0], high) + (dot(table[0], low) + dot(table[1], high))


def times(a, b):
    n = a.shape[0] // 2
    ar, ai, br, bi = a[:n], a[n:], b[:n], b[n:]
    return jnp.concatenate((ar * br - ai * bi, ar * bi + ai * br))


def shifted(a):
    q = a.shape[0] // 4
    return jnp.concatenate((a[:q], -a[q : 2 * q], a[2 * q : 3 * q], -a[3 * q :]))


def pack_kernel(l_ref, g_ref, o_ref):
    for k in range(2):
        for p in range(2):
            o_ref[0, k, p] = l_ref[k, p]
            o_ref[0, k, 2 + p] = g_ref[k, p]


def correlate_kernel(left_ref, right_ref, back_ref, x_ref, o_ref):
    half = x_ref.shape[0] // 2
    width = x_ref.shape[4]

    def pair(part, first):
        re = x_ref[part * half : (part + 1) * half, 0, first]
        im = x_ref[part * half : (part + 1) * half, 0, first + 1]
        return jnp.concatenate((re.reshape(half * 8, width), im.reshape(half * 8, width)))

    l_low, l_high = dot3(left_ref, pair(0, 0)), dot3(left_ref, pair(1, 0))
    r_low, r_high = dot3(right_ref, pair(0, 2)), dot3(right_ref, pair(1, 2))
    low = times(l_low, r_low) + times(l_high, shifted(r_low) + r_high)
    high = times(l_high, r_low)
    for part, joint in enumerate((low, high)):
        out = dot3(back_ref, joint)
        o_ref[part * half : (part + 1) * half, 0, 0] = out[: half * 8].reshape(half, 8, width)
        o_ref[part * half : (part + 1) * half, 0, 1] = out[half * 8 :].reshape(half, 8, width)


def finish_kernel(pattern_ref, v_ref, x_ref, pol_ref, scr_ref, xh, xl):
    groups, rows, low_energy, piece = x_ref.shape
    columns = groups * piece // (NB * NR)
    per = piece // NR
    m = rows * low_energy
    for g in range(groups):
        pol_ref[:, :, g * piece : (g + 1) * piece] = x_ref[g]
    for c in range(columns):
        for b in range(NB):
            at = c * NB + pattern_ref[c, b]
            lane = pl.multiple_of((at % per) * NR, NR)
            high, low = split(x_ref[at // per, :, :, pl.ds(lane, NR)].reshape(m, NR))
            xh[c * m : (c + 1) * m, b * NR : (b + 1) * NR] = high
            xl[c * m : (c + 1) * m, b * NR : (b + 1) * NR] = low
    dot = functools.partial(
        lax.dot_general, dimension_numbers=(((1,), (1,)), ((), ())), preferred_element_type=F32
    )
    total = jnp.zeros((columns * m, NR), F32)
    for b in range(NB):
        cut = slice(b * NR, (b + 1) * NR)
        vh, vl = split(v_ref[b])
        total += dot(xh[:, cut], vh) + (dot(xl[:, cut], vh) + dot(xh[:, cut], vl))
    for c in range(columns):
        scr_ref[:, :, c * NR : (c + 1) * NR] = total[c * m : (c + 1) * m].reshape(rows, low_energy, NR)


def broadcast_panels(panel_store, owner):
    me = lax.axis_index("m")
    rows = NR // 8
    part = lax.axis_index(("y", "c"))
    mine = lax.dynamic_slice_in_dim(panel_store, part * rows, rows, 1)
    mine = jnp.where((owner == me)[:, None, None], mine, 0.0)
    mine = lax.psum(mine, "m")
    return lax.all_gather(mine, ("y", "c"), axis=1, tiled=True)


def local(lesser, greater_t, panel_store, owner, pattern):
    kpoints, _, local_energy, elements = lesser.shape
    axes = ("z", "y", "c")
    groups = lax.axis_size(axes)
    total_energy = groups * local_energy
    piece = elements // groups
    tables = make_tables(total_energy // 2, 1.0 / math.sqrt(total_energy))
    panels = broadcast_panels(panel_store, owner)

    packed = pl.pallas_call(
        pack_kernel,
        grid=(groups,),
        in_specs=[pl.BlockSpec((kpoints, 2, local_energy, piece), lambda j: (0, 0, 0, j))] * 2,
        out_specs=pl.BlockSpec((1, kpoints, 4, local_energy, piece), lambda j: (j, 0, 0, 0, 0)),
        out_shape=jax.ShapeDtypeStruct((groups, kpoints, 4, local_energy, piece), F32),
        name="pack",
    )(lesser, greater_t)
    pieces = lax.all_to_all(packed, axes, 0, 0, tiled=True)
    pieces, panels = lax.optimization_barrier((pieces, panels))

    width = 256
    whole = lambda t: pl.BlockSpec(t.shape, lambda k, j: (0,) * t.ndim)
    result = pl.pallas_call(
        correlate_kernel,
        grid=(kpoints, piece // width),
        in_specs=[whole(t) for t in tables]
        + [pl.BlockSpec((groups, 1, 4, local_energy, width), lambda k, j: (0, k, 0, 0, j))],
        out_specs=pl.BlockSpec((groups, 1, 2, local_energy, width), lambda k, j: (0, k, 0, 0, j)),
        out_shape=jax.ShapeDtypeStruct((groups, kpoints, 2, local_energy, piece), F32),
        compiler_params=pltpu.CompilerParams(vmem_limit_bytes=40 * 2**20),
        name="correlate",
    )(*[jnp.asarray(t) for t in tables], pieces)
    returned = lax.all_to_all(result.reshape(groups, kpoints * 2, local_energy, piece), axes, 0, 0, tiled=True)

    columns = elements // (NB * NR)
    rows = kpoints * 2
    vmem = pl.BlockSpec(memory_space=pltpu.VMEM)
    polarization, screened = pl.pallas_call(
        finish_kernel,
        in_specs=[pl.BlockSpec(memory_space=pltpu.SMEM), vmem, vmem],
        out_specs=[vmem, vmem],
        out_shape=[
            jax.ShapeDtypeStruct((rows, local_energy, elements), F32),
            jax.ShapeDtypeStruct((rows, local_energy, columns * NR), F32),
        ],
        scratch_shapes=[pltpu.VMEM((columns * rows * local_energy, NB * NR), BF16)] * 2,
        compiler_params=pltpu.CompilerParams(vmem_limit_bytes=40 * 2**20),
        name="finish",
    )(pattern, panels, returned)
    return (
        polarization.reshape(kpoints, 2, local_energy, elements),
        screened.reshape(kpoints, 2, local_energy, columns * NR),
    )


def solution(mesh):
    split_mesh = Mesh(mesh.devices.reshape(4, 4, 2, 8), ("z", "y", "c", "m"))
    energy = ("z", "y", "c")
    in_specs = (
        P(None, None, energy, "m"),
        P(None, None, energy, "m"),
        P("m", None, None),
        P(),
        P("m", None),
    )
    out_specs = (P(None, None, energy, "m"), P(None, None, energy, "m"))
    return jax.shard_map(local, mesh=split_mesh, in_specs=in_specs, out_specs=out_specs, check_vma=False)
```

time: 355 us -> 257 us (0.72)
  blocking collectives: 102 us -> 0 us
  matrix products: 62.1 us -> 0 us
  waiting for transfers between devices: 133 us -> 191 us
  Pallas kernels: 0 us -> 28.8 us
  local copies, waits for them, and re-layouts: 25.1 us -> 1.42 us
  starting transfers between devices: 6.06 us -> 17.8 us
    all_to_all x1 -> x0, blocking collectives: 102 us -> none  [local(): lax.all_to_all(stacked, 'energy', split_axis=2, concat_axis=1, tiled=True)]
    psum x1, waiting for transfers between devices: 49.8 us -> 118 us  [broadcast_panels(): mine = lax.psum(mine, 'm')]
    dot_general x13 -> x0, matrix products: 62.1 us -> none  [the longest x8 42.5 us: apply_table(): jnp.einsum('ft,ktm->kfm', table, values, precision=lax.Precision.HIGHEST)]
    all_to_all x1 -> x2, waiting for transfers between devices: 83.7 us -> 48.3 us  [the longest x1 48.3 us: local(): lax.all_to_all(result.reshape(groups, kpoints * 2, local_energy, piece),...]
    pallas_call x0 -> x3, Pallas kernels: none -> 28.8 us  [the longest x1 17.4 us: local(): pl.pallas_call(pack_kernel, grid=(groups,), in_specs=[pl.BlockSpec((kpoin...]
    all_gather x0 -> x1, waiting for transfers between devices: none -> 24.4 us  [broadcast_panels(): return lax.all_gather(mine, ('y', 'c'), axis=1, tiled=True)]
    all_to_all x1 -> x2, starting transfers between devices: 6.02 us -> 17.7 us  [the longest x1 9.33 us: local(): pieces = lax.all_to_all(packed, axes, 0, 0, tiled=True)]
    reshape x3 -> x0, local copies, waits for them, and re-layouts: 8.21 us -> none  [the longest x1 4.27 us: local(): result = result.reshape(kpoints * 2, total_energy, 1, count)]
  transfers between devices with their start and end apart: 2 -> 4, of which waited for: 2 -> 3; matrix products, arithmetic and copies ran while one was open for 4% -> 1% of each run, Pallas kernels for 0% -> 0%
where the time goes in v1:
time: 257 us; the launch traced here: 255 us
  waiting for transfers between devices  191 us (74%)
  Pallas kernels  28.8 us (11%)
  starting transfers between devices  17.8 us (7%)
  between operations  14.1 us (5%)
    psum x1, waiting for transfers between devices, broadcast_panels(): mine = lax.psum(mine, 'm')  118 us
    all_to_all x1, waiting for transfers between devices, local(): lax.all_to_all(result.reshape(groups, kpoints * 2, local_energy, piece),...  48.3 us
    all_gather x1, waiting for transfers between devices, broadcast_panels(): return lax.all_gather(mine, ('y', 'c'), axis=1, tiled=True)  24.4 us
    pallas_call x1, Pallas kernels, local(): pl.pallas_call(pack_kernel, grid=(groups,), in_specs=[pl.BlockSpec((kpoin...  17.4 us
    all_to_all x1, starting transfers between devices, local(): pieces = lax.all_to_all(packed, axes, 0, 0, tiled=True)  9.33 us
    all_to_all x1, starting transfers between devices, local(): lax.all_to_all(result.reshape(groups, kpoints * 2, local_energy, piece),...  8.35 us
    pallas_call x1, Pallas kernels, local(): pl.pallas_call(correlate_kernel, grid=(kpoints, piece // width), in_specs...  8.13 us
  transfers between devices with their start and end apart: 4, of which 3 were waited for; matrix products, arithmetic and copies ran while one was open for 1% of the time, Pallas kernels for 0%

profile of v1, /device:TPU:8, one launch (start us, length us, event | category | flops | bytes accessed | tf_op | source)
XLA Modules:
  0.0 254.7 jit_solution(5329800433622406288)
XLA Ops:
  7.2 17.4 %pack.1 = f32[32,2,4,8,512]{4,3,2,1,0:T(8,128)} custom-call(f32[2,2,8,16384]{3,2,1,0:T(8,128)} %l_ref.1, f32[2,2,8,16384]{3,2,1,0:T(8,128)} %g_ref.1), custom_call_target="tpu_custom_call" | custom-call | tf_op jit(solution)/shard_map/pack/pallas_call | solution.py:129
  24.5 0.0 copy-start.4
  24.6 9.3 %all-to-all-start = ((f32[32,2,4,8,512]{4,3,2,1,0:T(8,128)}), f32[32,2,4,8,512]{4,3,2,1,0:T(8,128)}, u32[]{:S(2)}, u32[]{:S(2)}) async-start(f32[32,2,4,8,512]{4,3,2,1,0:T(8,128)} %pack.1), calls=%async_computation | async-start | bytes 8388608 | tf_op jit(solution)/shard_map/all_to_all | solution.py:137
  33.9 0.0 all-reduce.2.cloned.1.call-start
  33.9 0.0 copy-done.6
  34.0 1.6 dynamic-slice_select_fusion
  35.6 0.0 all-reduce.2.cloned.1.call-update
  35.6 0.0 all-gather.2.cloned.1.call-start
  35.7 118.2 %all-reduce.2.cloned.1.call-done = f32[4,32,256]{2,1,0:T(8,128)} async-done(((f32[4,32,256]{2,1,0:T(8,128)}), f32[4,32,256]{2,1,0:T(8,128)}) %all-reduce.2.cloned.1.call-update) | async-done | bytes 131088 | tf_op jit(solution)/shard_map/psum | solution.py:116
  153.9 0.0 all-gather.2.cloned.1.call-update
  153.9 24.4 %all-gather.2.cloned.1.call-done.v_ref = f32[4,256,256]{2,1,0:T(8,128)} async-done(((f32[4,32,256]{2,1,0:T(8,128)}), f32[4,256,256]{2,1,0:T(8,128)}) %all-gather.2.cloned.1.call-update) | async-done | bytes 1048592 | tf_op jit(solution)/shard_map/all_gather | solution.py:117
  178.3 0.0 all-to-all-done.x_ref
  178.3 0.0 copy-done.2
  178.3 0.0 copy-done.3
  178.3 0.0 copy-done.4
  178.3 8.1 %correlate.1 = f32[32,2,2,8,512]{4,3,2,1,0:T(8,128)S(1)} custom-call(bf16[2,512,256]{2,1,0:T(8,128)(2,1)S(1)} %copy-done.2, bf16[2,512,256]{2,1,0:T(8,128)(2,1)S(1)} %copy-done.3, bf16[2,256,512]{2,1,0:T(8,128)(2,1)S(1)} %copy-done.4, f32[32,2,4,8,512]{4,3,2,1,0:T(8,128)} %all-to-all-done.x_ref), custom_call_target="tpu_custom_call" | custom-call | tf_op jit(solution)/shard_map/correlate/pallas_call | solution.py:142
  186.4 0.0 copy-start
  186.4 1.3 copy-done
  187.7 8.3 %all-to-all-start.1 = ((f32[32,4,8,512]{3,2,1,0:T(8,128)}), f32[32,4,8,512]{3,2,1,0:T(8,128)S(1)}, u32[]{:S(2)}, u32[]{:S(2)}) async-start(f32[32,4,8,512]{3,2,1,0:T(8,128)} %bitcast.3), calls=%async_computation.1 | async-start | bytes 4194304 | tf_op jit(solution)/shard_map/all_to_all | solution.py:152
  196.1 0.0 copy-done.5
  196.1 0.1 copy.10.pattern_ref
  196.2 48.3 %all-to-all-done.1.x_ref = f32[32,4,8,512]{3,2,1,0:T(8,128)S(1)} async-done(((f32[32,4,8,512]{3,2,1,0:T(8,128)}), f32[32,4,8,512]{3,2,1,0:T(8,128)S(1)}, u32[]{:S(2)}, u32[]{:S(2)}) %all-to-all-start.1) | async-done | bytes 2097184 | tf_op jit(solution)/shard_map/all_to_all | solution.py:152
  244.5 0.0 copy-done.1
  244.5 3.3 %finish.1 = (f32[4,8,16384]{2,1,0:T(8,128)}, f32[4,8,4096]{2,1,0:T(8,128)}) custom-call(s32[16,4]{1,0:T(8,128)S(1)} %copy.10.pattern_ref, f32[4,256,256]{2,1,0:T(8,128)S(1)} %copy-done.1, f32[32,4,8,512]{3,2,1,0:T(8,128)S(1)} %all-to-all-done.1.x_ref), custom_call_target="tpu_custom_call" | custom-call | tf_op jit(solution)/shard_map/finish/pallas_call | solution.py:157
  (6 shorter events, 0.0 us)
Async XLA Ops:
  24.5 9.4 %copy-start.6 = (s32[4]{0:T(128)S(1)}, s32[4]{0:T(128)}, u32[]{:S(2)}) copy-start(s32[4]{0:T(128)} %param.11) | copy-start | bytes 52
  24.5 153.7 %copy-start.2 = (bf16[2,512,256]{2,1,0:T(8,128)(2,1)S(1)}, bf16[2,512,256]{2,1,0:T(8,128)(2,1)}, u32[]{:S(2)}) copy-start(bf16[2,512,256]{2,1,0:T(8,128)(2,1)} %constant.30.clone.left_ref) | copy-start | bytes 1572868
  24.5 153.7 %copy-start.3 = (bf16[2,512,256]{2,1,0:T(8,128)(2,1)S(1)}, bf16[2,512,256]{2,1,0:T(8,128)(2,1)}, u32[]{:S(2)}) copy-start(bf16[2,512,256]{2,1,0:T(8,128)(2,1)} %constant.31.clone.right_ref) | copy-start | bytes 1572868
  24.5 153.7 %copy-start.4 = (bf16[2,256,512]{2,1,0:T(8,128)(2,1)S(1)}, bf16[2,256,512]{2,1,0:T(8,128)(2,1)}, u32[]{:S(2)}) copy-start(bf16[2,256,512]{2,1,0:T(8,128)(2,1)} %constant.32.clone.back_ref) | copy-start | bytes 1572868
  24.6 153.7 %all-to-all-start = ((f32[32,2,4,8,512]{4,3,2,1,0:T(8,128)}), f32[32,2,4,8,512]{4,3,2,1,0:T(8,128)}, u32[]{:S(2)}, u32[]{:S(2)}) async-start(f32[32,2,4,8,512]{4,3,2,1,0:T(8,128)} %pack.1), calls=%async_computation | async-start | bytes 8388608 | tf_op jit(solution)/shard_map/all_to_all | solution.py:137
  33.9 120.0 %all-reduce.2.cloned.1.call-start = ((), (), s32[]{:S(2)}) async-start(), calls=%async_computation.2 | async-start | bytes 262144 | tf_op jit(solution)/shard_map/psum | solution.py:116
  35.6 142.6 %all-gather.2.cloned.1.call-start = ((), (), s32[]{:S(2)}) async-start(), calls=%async_computation.3 | async-start | bytes 1179648 | tf_op jit(solution)/shard_map/all_gather | solution.py:117
  186.4 1.3 copy-start
  187.7 8.4 %copy-start.5 = (s32[16,4]{0,1:T(4,128)S(1)}, s32[16,4]{0,1:T(4,128)}, u32[]{:S(2)}) copy-start(s32[16,4]{0,1:T(4,128)} %param.12) | copy-start | bytes 772
  187.7 56.8 %copy-start.1 = (f32[4,256,256]{2,1,0:T(8,128)S(1)}, f32[4,256,256]{2,1,0:T(8,128)}, u32[]{:S(2)}) copy-start(f32[4,256,256]{2,1,0:T(8,128)} %all-gather.2.cloned.1.call-done.v_ref) | copy-start | bytes 3145732
  187.7 56.8 %all-to-all-start.1 = ((f32[32,4,8,512]{3,2,1,0:T(8,128)}), f32[32,4,8,512]{3,2,1,0:T(8,128)S(1)}, u32[]{:S(2)}, u32[]{:S(2)}) async-start(f32[32,4,8,512]{3,2,1,0:T(8,128)} %bitcast.3), calls=%async_computation.1 | async-start | bytes 4194304 | tf_op jit(solution)/shard_map/all_to_all | solution.py:152
Sparse Core Ops, SparseCore 0:
  37.9 115.9 all-reduce.1
  155.9 22.3 all-gather.1

commit v2 on v1

v2 whole, which is shorter than its diff:
```python
import functools
import math

import jax
import jax.numpy as jnp
import ml_dtypes
import numpy as np
from jax import lax
from jax.experimental import pallas as pl
from jax.experimental.pallas import tpu as pltpu
from jax.sharding import Mesh, PartitionSpec as P

NB = 4
NR = 256
F32 = jnp.float32
BF16 = jnp.bfloat16


def split_table(table):
    high = table.astype(ml_dtypes.bfloat16)
    low = (table - high.astype(np.float64)).astype(ml_dtypes.bfloat16)
    return np.stack((high, low))


def make_tables(block, scale):
    length = 2 * block
    freq = np.concatenate((np.arange(0, length, 2), np.arange(1, length, 2)))
    angle = (freq[:, None] * np.arange(block)[None, :] % length) * (2.0 * math.pi / length)
    cosine, sine = np.cos(angle), np.sin(angle)
    left = np.block([[cosine, sine], [-sine, cosine]])
    right = np.block([[cosine, -sine], [sine, cosine]])
    back = np.block([[sine.T, cosine.T], [-cosine.T, sine.T]]) * (scale / length)
    return split_table(left), split_table(right), split_table(back)


def split(values):
    high = values.astype(BF16)
    return high, (values - high.astype(F32)).astype(BF16)


def dot3(table, values):
    high, low = split(values)
    dot = functools.partial(jnp.dot, preferred_element_type=F32)
    return dot(table[0], high) + (dot(table[0], low) + dot(table[1], high))


def times(a, b):
    n = a.shape[0] // 2
    ar, ai, br, bi = a[:n], a[n:], b[:n], b[n:]
    return jnp.concatenate((ar * br - ai * bi, ar * bi + ai * br))


def shifted(a):
    q = a.shape[0] // 4
    return jnp.concatenate((a[:q], -a[q : 2 * q], a[2 * q : 3 * q], -a[3 * q :]))


def pack_kernel(l_ref, g_ref, o_ref, held, read_sems, write_sems):
    groups, _, _, _, piece = o_ref.shape
    reads = [
        pltpu.make_async_copy(
            ref.at[:, :, :, j * piece : (j + 1) * piece],
            held.at[j, :, 2 * side : 2 * side + 2],
            read_sems.at[2 * j + side],
        )
        for j in range(groups)
        for side, ref in enumerate((l_ref, g_ref))
    ]
    writes = [pltpu.make_async_copy(held.at[j], o_ref.at[j], write_sems.at[j]) for j in range(groups)]
    for copy in reads:
        copy.start()
    for j, copy in enumerate(writes):
        reads[2 * j].wait()
        reads[2 * j + 1].wait()
        copy.start()
    for copy in writes:
        copy.wait()


def correlate_kernel(left_ref, right_ref, back_ref, x_ref, o_ref):
    groups, kpoints, _, rows, piece = x_ref.shape
    half = groups // 2
    width = min(256, piece)
    for k in range(kpoints):
        for start in range(0, piece, width):
            lanes = slice(start, start + width)

            def pair(part, first):
                cut = slice(part * half, (part + 1) * half)
                re, im = x_ref[cut, k, first, :, lanes], x_ref[cut, k, first + 1, :, lanes]
                return jnp.concatenate((re.reshape(half * rows, width), im.reshape(half * rows, width)))

            l_low, l_high = dot3(left_ref, pair(0, 0)), dot3(left_ref, pair(1, 0))
            r_low, r_high = dot3(right_ref, pair(0, 2)), dot3(right_ref, pair(1, 2))
            low = times(l_low, r_low) + times(l_high, shifted(r_low) + r_high)
            high = times(l_high, r_low)
            for part, joint in enumerate((low, high)):
                out = dot3(back_ref, joint)
                cut = slice(part * half, (part + 1) * half)
                o_ref[cut, 2 * k, :, lanes] = out[: half * rows].reshape(half, rows, width)
                o_ref[cut, 2 * k + 1, :, lanes] = out[half * rows :].reshape(half, rows, width)


def finish_kernel(pattern_ref, v_ref, x_ref, pol_ref, scr_ref, xh, xl, sems):
    groups, rows, low_energy, piece = x_ref.shape
    columns = groups * piece // (NB * NR)
    per = piece // NR
    m = rows * low_energy
    copies = [
        pltpu.make_async_copy(x_ref.at[g], pol_ref.at[:, :, g * piece : (g + 1) * piece], sems.at[g])
        for g in range(groups)
    ]
    for copy in copies:
        copy.start()
    for c in range(columns):
        for b in range(NB):
            at = c * NB + pattern_ref[c, b]
            lane = pl.multiple_of((at % per) * NR, NR)
            high, low = split(x_ref[at // per, :, :, pl.ds(lane, NR)].reshape(m, NR))
            xh[c * m : (c + 1) * m, b * NR : (b + 1) * NR] = high
            xl[c * m : (c + 1) * m, b * NR : (b + 1) * NR] = low
    dot = functools.partial(
        lax.dot_general, dimension_numbers=(((1,), (1,)), ((), ())), preferred_element_type=F32
    )
    total = jnp.zeros((columns * m, NR), F32)
    for b in range(NB):
        cut = slice(b * NR, (b + 1) * NR)
        vh, vl = split(v_ref[b])
        total += dot(xh[:, cut], vh) + (dot(xl[:, cut], vh) + dot(xh[:, cut], vl))
    for c in range(columns):
        scr_ref[:, :, c * NR : (c + 1) * NR] = total[c * m : (c + 1) * m].reshape(rows, low_energy, NR)
    for copy in copies:
        copy.wait()


def partial_panels(panel_store, owner):
    me = lax.axis_index(("x", "g"))
    at = lax.axis_index("x")
    size = lax.axis_size("x")
    rows = NR // (8 * size)
    part = lax.axis_index(("y", "c"))
    mine = lax.dynamic_index_in_dim(panel_store.reshape(NB, size, 8, rows, NR), part, 2, keepdims=False)
    mine = jnp.where((owner == me)[:, None, None, None], mine, 0.0)
    total = lax.dynamic_index_in_dim(mine, at, 1, keepdims=False)
    for step in range(1, size):
        piece = lax.dynamic_index_in_dim(mine, (at + step) % size, 1, keepdims=False)
        total = total + lax.ppermute(piece, "x", [(i, (i + step) % size) for i in range(size)])
    total = total + lax.ppermute(total, "g", [(0, 1), (1, 0)])
    return lax.all_gather(total, ("y", "c"), axis=1, tiled=True)


def whole_panels(rows):
    at = lax.axis_index("x")
    size = lax.axis_size("x")
    share = rows.shape[1]
    panels = jnp.zeros((NB, NR, NR), F32)
    panels = lax.dynamic_update_slice_in_dim(panels, rows, at * share, 1)
    for step in range(1, size):
        piece = lax.ppermute(rows, "x", [(i, (i + step) % size) for i in range(size)])
        panels = lax.dynamic_update_slice_in_dim(panels, piece, (at - step) % size * share, 1)
    return panels


def local(lesser, greater_t, panel_store, owner, pattern):
    kpoints, _, local_energy, elements = lesser.shape
    axes = ("z", "y", "c")
    groups = lax.axis_size(axes)
    total_energy = groups * local_energy
    piece = elements // groups
    tables = make_tables(total_energy // 2, 1.0 / math.sqrt(total_energy))
    panel_rows = partial_panels(panel_store, owner)
    vmem = pl.BlockSpec(memory_space=pltpu.VMEM)
    hbm = pl.BlockSpec(memory_space=pltpu.HBM)
    params = pltpu.CompilerParams(vmem_limit_bytes=24 * 2**20)

    packed = pl.pallas_call(
        pack_kernel,
        in_specs=[hbm, hbm],
        out_specs=hbm,
        out_shape=jax.ShapeDtypeStruct((groups, kpoints, 4, local_energy, piece), F32),
        scratch_shapes=[
            pltpu.VMEM((groups, kpoints, 4, local_energy, piece), F32),
            pltpu.SemaphoreType.DMA((2 * groups,)),
            pltpu.SemaphoreType.DMA((groups,)),
        ],
        compiler_params=pltpu.CompilerParams(vmem_limit_bytes=60 * 2**20),
        name="pack",
    )(lesser, greater_t)
    pieces = lax.all_to_all(packed, axes, 0, 0, tiled=True)
    pieces, panel_rows = lax.optimization_barrier((pieces, panel_rows))
    panels = whole_panels(panel_rows)

    rows = kpoints * 2
    result = pl.pallas_call(
        correlate_kernel,
        in_specs=[vmem] * 4,
        out_specs=vmem,
        out_shape=jax.ShapeDtypeStruct((groups, rows, local_energy, piece), F32),
        compiler_params=params,
        name="correlate",
    )(*[jnp.asarray(t) for t in tables], pieces)
    returned = lax.all_to_all(result, axes, 0, 0, tiled=True)

    columns = elements // (NB * NR)
    polarization, screened = pl.pallas_call(
        finish_kernel,
        in_specs=[pl.BlockSpec(memory_space=pltpu.SMEM), vmem, vmem],
        out_specs=[hbm, vmem],
        out_shape=[
            jax.ShapeDtypeStruct((rows, local_energy, elements), F32),
            jax.ShapeDtypeStruct((rows, local_energy, columns * NR), F32),
        ],
        scratch_shapes=[pltpu.VMEM((columns * rows * local_energy, NB * NR), BF16)] * 2
        + [pltpu.SemaphoreType.DMA((groups,))],
        compiler_params=params,
        name="finish",
    )(pattern, panels, returned)
    return (
        polarization.reshape(kpoints, 2, local_energy, elements),
        screened.reshape(kpoints, 2, local_energy, columns * NR),
    )


def solution(mesh):
    split_mesh = Mesh(mesh.devices.reshape(4, 4, 2, 4, 2), ("z", "y", "c", "x", "g"))
    energy, matrix = ("z", "y", "c"), ("x", "g")
    in_specs = (
        P(None, None, energy, matrix),
        P(None, None, energy, matrix),
        P(matrix, None, None),
        P(),
        P(matrix, None),
    )
    out_specs = (P(None, None, energy, matrix), P(None, None, energy, matrix))
    return jax.shard_map(local, mesh=split_mesh, in_specs=in_specs, out_specs=out_specs, check_vma=False)
```

time: 257 us -> 181 us (0.70)
  waiting for transfers between devices: 191 us -> 110 us
  starting transfers between devices: 17.8 us -> 32 us
  blocking collectives: 0 us -> 13.3 us
  between operations: 14.1 us -> 0.86 us
  Pallas kernels: 28.8 us -> 17.1 us
  local copies, waits for them, and re-layouts: 1.42 us -> 5.72 us
    psum x1 -> x0, waiting for transfers between devices: 118 us -> none  [broadcast_panels(): mine = lax.psum(mine, 'm')]
    ppermute x0 -> x7, waiting for transfers between devices: none -> 73.4 us  [the longest x1 61.5 us: partial_panels(): total = total + lax.ppermute(total, 'g', [(0, 1), (1, 0)])]
    all_gather x1 -> x0, waiting for transfers between devices: 24.4 us -> none  [broadcast_panels(): return lax.all_gather(mine, ('y', 'c'), axis=1, tiled=True)]
    all_to_all x1, waiting for transfers between devices: 48.3 us -> 30 us  [local(): returned = lax.all_to_all(result, axes, 0, 0, tiled=True)]
    ppermute x0 -> x7, starting transfers between devices: none -> 16.1 us  [the longest x3 5.78 us: whole_panels(): lax.ppermute(rows, 'x', [(i, (i + step) % size) for i in range(size)])]
    all_gather x0 -> x1, blocking collectives: none -> 13.3 us  [partial_panels(): return lax.all_gather(total, ('y', 'c'), axis=1, tiled=True)]
    pallas_call x2, Pallas kernels: 25.5 us -> 13.3 us  [the longest x1 8.25 us: local(): pl.pallas_call(correlate_kernel, in_specs=[vmem] * 4, out_specs=vmem, out...]
    all_to_all x1, waiting for transfers between devices: 0.01 us -> 7 us  [local(): pieces = lax.all_to_all(packed, axes, 0, 0, tiled=True)]
  transfers between devices with their start and end apart: 4 -> 9, of which waited for: 3 -> 7; matrix products, arithmetic and copies ran while one was open for 1% -> 1% of each run, Pallas kernels for 0% -> 0%
where the time goes in v2:
time: 181 us; the launch traced here: 179 us
  waiting for transfers between devices  110 us (61%)
  starting transfers between devices  32 us (18%)
  Pallas kernels  17.1 us (9%)
  blocking collectives  13.3 us (7%)
  local copies, waits for them, and re-layouts  5.72 us (3%)
    ppermute x1, waiting for transfers between devices, partial_panels(): total = total + lax.ppermute(total, 'g', [(0, 1), (1, 0)])  61.5 us
    all_to_all x1, waiting for transfers between devices, local(): returned = lax.all_to_all(result, axes, 0, 0, tiled=True)  30 us
    all_gather x1, blocking collectives, partial_panels(): return lax.all_gather(total, ('y', 'c'), axis=1, tiled=True)  13.3 us
    ppermute x3, waiting for transfers between devices, whole_panels(): lax.ppermute(rows, 'x', [(i, (i + step) % size) for i in range(size)])  9.43 us
    all_to_all x1, starting transfers between devices, local(): pieces = lax.all_to_all(packed, axes, 0, 0, tiled=True)  9.34 us
    pallas_call x1, Pallas kernels, local(): pl.pallas_call(correlate_kernel, in_specs=[vmem] * 4, out_specs=vmem, out...  8.25 us
    all_to_all x1, waiting for transfers between devices, local(): pieces = lax.all_to_all(packed, axes, 0, 0, tiled=True)  7 us
    all_to_all x1, starting transfers between devices, local(): returned = lax.all_to_all(result, axes, 0, 0, tiled=True)  6.53 us
  transfers between devices with their start and end apart: 9, of which 7 were waited for; matrix products, arithmetic and copies ran while one was open for 1% of the time, Pallas kernels for 0%

profile of v2, /device:TPU:8, one launch (start us, length us, event | category | flops | bytes accessed | tf_op | source)
XLA Modules:
  0.0 179.5 jit_solution(8591014035273327886)
XLA Ops:
  0.6 5.0 %pack.1 = f32[32,2,4,8,512]{4,3,2,1,0:T(8,128)} custom-call(f32[2,2,8,16384]{3,2,1,0:T(8,128)} %l_ref.1, f32[2,2,8,16384]{3,2,1,0:T(8,128)} %g_ref.1), custom_call_target="tpu_custom_call" | custom-call | tf_op jit(solution)/shard_map/pack/pallas_call | solution.py:176
  5.7 9.3 %all-to-all-start = ((f32[32,2,4,8,512]{4,3,2,1,0:T(8,128)}), f32[32,2,4,8,512]{4,3,2,1,0:T(8,128)}, u32[]{:S(2)}, u32[]{:S(2)}) async-start(f32[32,2,4,8,512]{4,3,2,1,0:T(8,128)} %pack.1), calls=%async_computation | async-start | bytes 8388608 | tf_op jit(solution)/shard_map/all_to_all | solution.py:189
  15.2 1.6 collective-permute-start
  16.8 2.7 %collective-permute-start.1 = (f32[4,8,256]{2,1,0:T(8,128)S(1)}, f32[4,8,256]{2,1,0:T(8,128)S(1)}, u32[]{:S(2)}, u32[]{:S(2)}) collective-permute-start(f32[4,8,256]{2,1,0:T(8,128)S(1)} %get-tuple-element.12), channel_id=1, source_target_pairs={{0,4},{2,6},{4,0},{6,2},{1,5},{3,7},{5,1},{7,3},{8,12},{10,14},{12... | collective-permute-start | bytes 98312 | tf_op jit(solution)/shard_map/ppermute | solution.py:147
  19.5 1.4 collective-permute-start.2
  21.0 1.3 collective-permute-done.1
  22.2 1.2 collective-permute-done.2
  23.5 4.6 %collective-permute-start.3 = (f32[4,8,256]{2,1,0:T(8,128)S(1)}, f32[4,8,256]{2,1,0:T(8,128)S(1)}, u32[]{:S(2)}, u32[]{:S(2)}) collective-permute-start(f32[4,8,256]{2,1,0:T(8,128)S(1)} %fusion.1), channel_id=1, source_target_pairs={{0,1},{1,0},{2,3},{3,2},{4,5},{5,4},{6,7},{7,6},{8,9},{9,8},{10,11... | collective-permute-start | bytes 98312 | tf_op jit(solution)/shard_map/ppermute | solution.py:148
  28.0 61.5 %collective-permute-done.3 = f32[4,8,256]{2,1,0:T(8,128)S(1)} collective-permute-done((f32[4,8,256]{2,1,0:T(8,128)S(1)}, f32[4,8,256]{2,1,0:T(8,128)S(1)}, u32[]{:S(2)}, u32[]{:S(2)}) %collective-permute-start.3) | collective-permute-done | bytes 32800 | tf_op jit(solution)/shard_map/ppermute | solution.py:148
  89.6 13.3 %all_gather.3 = f32[4,64,256]{2,1,0:T(8,128)S(1)} all-gather(f32[4,8,256]{2,1,0:T(8,128)S(1)} %add.94), channel_id=1, replica_groups=mesh['z'=4,'y'=4,'c'=2,'x'=4,'g'=2] {'y','c'}, dimensions={1}, use_global_device_ids=true | all-gather | bytes 294912 | tf_op jit(solution)/shard_map/all_gather | solution.py:149
  102.8 7.0 %all-to-all-done.x_ref = f32[32,2,4,8,512]{4,3,2,1,0:T(8,128)} async-done(((f32[32,2,4,8,512]{4,3,2,1,0:T(8,128)}), f32[32,2,4,8,512]{4,3,2,1,0:T(8,128)}, u32[]{:S(2)}, u32[]{:S(2)}) %all-to-all-start) | async-done | bytes 4194336 | tf_op jit(solution)/shard_map/all_to_all | solution.py:189
  109.9 8.3 %correlate.1 = f32[32,4,8,512]{3,2,1,0:T(8,128)S(1)} custom-call(bf16[2,512,256]{2,1,0:T(8,128)(2,1)S(1)} %copy-done.4, bf16[2,512,256]{2,1,0:T(8,128)(2,1)S(1)} %copy-done.5, bf16[2,256,512]{2,1,0:T(8,128)(2,1)S(1)} %copy-done.6, f32[32,2,4,8,512]{4,3,2,1,0:T(8,128)} %all-to-all-done.x_ref), custom_call_target="tpu_custom_call" | custom-call | tf_op jit(solution)/shard_map/correlate/pallas_call | solution.py:194
  118.1 1.3 copy-done.1
  119.4 6.5 %all-to-all-start.1 = ((f32[32,4,8,512]{3,2,1,0:T(8,128)}), f32[32,4,8,512]{3,2,1,0:T(8,128)S(1)}, u32[]{:S(2)}, u32[]{:S(2)}) async-start(f32[32,4,8,512]{3,2,1,0:T(8,128)} %copy-done.1), calls=%async_computation.1 | async-start | bytes 4194304 | tf_op jit(solution)/shard_map/all_to_all | solution.py:202
  126.0 1.6 collective-permute-start.4
  127.6 2.7 %collective-permute-start.5 = (f32[4,64,256]{2,1,0:T(8,128)S(1)}, f32[4,64,256]{2,1,0:T(8,128)}, u32[]{:S(2)}, u32[]{:S(2)}) collective-permute-start(f32[4,64,256]{2,1,0:T(8,128)S(1)} %all_gather.3), channel_id=1, source_target_pairs={{0,4},{2,6},{4,0},{6,2},{1,5},{3,7},{5,1},{7,3},{8,12},{10,14},{12... | collective-permute-start | bytes 786440 | tf_op jit(solution)/shard_map/ppermute | solution.py:159
  130.4 1.5 collective-permute-start.6
  132.0 3.8 %collective-permute-done.4 = f32[4,64,256]{2,1,0:T(8,128)} collective-permute-done((f32[4,64,256]{2,1,0:T(8,128)S(1)}, f32[4,64,256]{2,1,0:T(8,128)}, u32[]{:S(2)}, u32[]{:S(2)}) %collective-permute-start.4) | collective-permute-done | bytes 262176 | tf_op jit(solution)/shard_map/ppermute | solution.py:159
  135.7 1.0 constant_dynamic-update-slice_fusion.2
  136.7 5.7 %collective-permute-done.5 = f32[4,64,256]{2,1,0:T(8,128)} collective-permute-done((f32[4,64,256]{2,1,0:T(8,128)S(1)}, f32[4,64,256]{2,1,0:T(8,128)}, u32[]{:S(2)}, u32[]{:S(2)}) %collective-permute-start.5) | collective-permute-done | bytes 262176 | tf_op jit(solution)/shard_map/ppermute | solution.py:159
  143.4 1.0 copy-done.2
  144.4 30.0 %all-to-all-done.1.x_ref = f32[32,4,8,512]{3,2,1,0:T(8,128)S(1)} async-done(((f32[32,4,8,512]{3,2,1,0:T(8,128)}), f32[32,4,8,512]{3,2,1,0:T(8,128)S(1)}, u32[]{:S(2)}, u32[]{:S(2)}) %all-to-all-start.1) | async-done | bytes 2097184 | tf_op jit(solution)/shard_map/all_to_all | solution.py:202
  174.4 1.2 copy-done.3
  175.6 3.9 %finish.1 = (f32[4,8,16384]{2,1,0:T(8,128)}, f32[4,8,4096]{2,1,0:T(8,128)}) custom-call(s32[16,4]{1,0:T(8,128)S(1)} %copy.11.pattern_ref, f32[4,256,256]{2,1,0:T(8,128)S(1)} %copy-done.3, f32[32,4,8,512]{3,2,1,0:T(8,128)S(1)} %all-to-all-done.1.x_ref), custom_call_target="tpu_custom_call" | custom-call | tf_op jit(solution)/shard_map/finish/pallas_call | solution.py:205
  (27 shorter events, 1.4 us)
Async XLA Ops:
  0.6 14.5 %copy-start = (f32[4,256,256]{2,1,0:T(8,128)S(1)}, f32[4,256,256]{2,1,0:T(8,128)}, u32[]{:S(2)}) copy-start(f32[4,256,256]{2,1,0:T(8,128)} %param.10) | copy-start | bytes 3145732
  5.7 9.4 %copy-start.8 = (s32[4]{0:T(128)S(1)}, s32[4]{0:T(128)}, u32[]{:S(2)}) copy-start(s32[4]{0:T(128)} %param.11) | copy-start | bytes 52
  5.7 104.2 %copy-start.4 = (bf16[2,512,256]{2,1,0:T(8,128)(2,1)S(1)}, bf16[2,512,256]{2,1,0:T(8,128)(2,1)}, u32[]{:S(2)}) copy-start(bf16[2,512,256]{2,1,0:T(8,128)(2,1)} %constant.88.clone.left_ref) | copy-start | bytes 1572868
  5.7 104.2 %copy-start.5 = (bf16[2,512,256]{2,1,0:T(8,128)(2,1)S(1)}, bf16[2,512,256]{2,1,0:T(8,128)(2,1)}, u32[]{:S(2)}) copy-start(bf16[2,512,256]{2,1,0:T(8,128)(2,1)} %constant.89.clone.right_ref) | copy-start | bytes 1572868
  5.7 104.2 %copy-start.6 = (bf16[2,256,512]{2,1,0:T(8,128)(2,1)S(1)}, bf16[2,256,512]{2,1,0:T(8,128)(2,1)}, u32[]{:S(2)}) copy-start(bf16[2,256,512]{2,1,0:T(8,128)(2,1)} %constant.90.clone.back_ref) | copy-start | bytes 1572868
  5.7 104.1 %all-to-all-start = ((f32[32,2,4,8,512]{4,3,2,1,0:T(8,128)}), f32[32,2,4,8,512]{4,3,2,1,0:T(8,128)}, u32[]{:S(2)}, u32[]{:S(2)}) async-start(f32[32,2,4,8,512]{4,3,2,1,0:T(8,128)} %pack.1), calls=%async_computation | async-start | bytes 8388608 | tf_op jit(solution)/shard_map/all_to_all | solution.py:189
  15.2 5.7 %collective-permute-start = (f32[4,8,256]{2,1,0:T(8,128)S(1)}, f32[4,8,256]{2,1,0:T(8,128)S(1)}, u32[]{:S(2)}, u32[]{:S(2)}) collective-permute-start(f32[4,8,256]{2,1,0:T(8,128)S(1)} %get-tuple-element.10), channel_id=1, source_target_pairs={{0,2},{2,4},{4,6},{6,0},{1,3},{3,5},{5,7},{7,1},{8,10},{10,12},{12... | collective-permute-start | bytes 98312 | tf_op jit(solution)/shard_map/ppermute | solution.py:147
  16.8 5.4 %collective-permute-start.1 = (f32[4,8,256]{2,1,0:T(8,128)S(1)}, f32[4,8,256]{2,1,0:T(8,128)S(1)}, u32[]{:S(2)}, u32[]{:S(2)}) collective-permute-start(f32[4,8,256]{2,1,0:T(8,128)S(1)} %get-tuple-element.12), channel_id=1, source_target_pairs={{0,4},{2,6},{4,0},{6,2},{1,5},{3,7},{5,1},{7,3},{8,12},{10,14},{12... | collective-permute-start | bytes 98312 | tf_op jit(solution)/shard_map/ppermute | solution.py:147
  19.5 3.9 %collective-permute-start.2 = (f32[4,8,256]{2,1,0:T(8,128)S(1)}, f32[4,8,256]{2,1,0:T(8,128)S(1)}, u32[]{:S(2)}, u32[]{:S(2)}) collective-permute-start(f32[4,8,256]{2,1,0:T(8,128)S(1)} %get-tuple-element.11), channel_id=1, source_target_pairs={{0,6},{2,0},{4,2},{6,4},{1,7},{3,1},{5,3},{7,5},{8,14},{10,8},{12,... | collective-permute-start | bytes 98312 | tf_op jit(solution)/shard_map/ppermute | solution.py:147
  23.5 66.1 %collective-permute-start.3 = (f32[4,8,256]{2,1,0:T(8,128)S(1)}, f32[4,8,256]{2,1,0:T(8,128)S(1)}, u32[]{:S(2)}, u32[]{:S(2)}) collective-permute-start(f32[4,8,256]{2,1,0:T(8,128)S(1)} %fusion.1), channel_id=1, source_target_pairs={{0,1},{1,0},{2,3},{3,2},{4,5},{5,4},{6,7},{7,6},{8,9},{9,8},{10,11... | collective-permute-start | bytes 98312 | tf_op jit(solution)/shard_map/ppermute | solution.py:148
  118.1 1.3 copy-start.1
  119.4 10.9 %copy-start.7 = (s32[16,4]{0,1:T(4,128)S(1)}, s32[16,4]{0,1:T(4,128)}, u32[]{:S(2)}) copy-start(s32[16,4]{0,1:T(4,128)} %param.12) | copy-start | bytes 772
  119.4 54.9 %all-to-all-start.1 = ((f32[32,4,8,512]{3,2,1,0:T(8,128)}), f32[32,4,8,512]{3,2,1,0:T(8,128)S(1)}, u32[]{:S(2)}, u32[]{:S(2)}) async-start(f32[32,4,8,512]{3,2,1,0:T(8,128)} %copy-done.1), calls=%async_computation.1 | async-start | bytes 4194304 | tf_op jit(solution)/shard_map/all_to_all | solution.py:202
  126.0 9.8 %collective-permute-start.4 = (f32[4,64,256]{2,1,0:T(8,128)S(1)}, f32[4,64,256]{2,1,0:T(8,128)}, u32[]{:S(2)}, u32[]{:S(2)}) collective-permute-start(f32[4,64,256]{2,1,0:T(8,128)S(1)} %all_gather.3), channel_id=1, source_target_pairs={{0,2},{2,4},{4,6},{6,0},{1,3},{3,5},{5,7},{7,1},{8,10},{10,12},{12... | collective-permute-start | bytes 786440 | tf_op jit(solution)/shard_map/ppermute | solution.py:159
  127.6 14.8 %collective-permute-start.5 = (f32[4,64,256]{2,1,0:T(8,128)S(1)}, f32[4,64,256]{2,1,0:T(8,128)}, u32[]{:S(2)}, u32[]{:S(2)}) collective-permute-start(f32[4,64,256]{2,1,0:T(8,128)S(1)} %all_gather.3), channel_id=1, source_target_pairs={{0,4},{2,6},{4,0},{6,2},{1,5},{3,7},{5,1},{7,3},{8,12},{10,14},{12... | collective-permute-start | bytes 786440 | tf_op jit(solution)/shard_map/ppermute | solution.py:159
  130.4 12.9 %collective-permute-start.6 = (f32[4,64,256]{2,1,0:T(8,128)S(1)}, f32[4,64,256]{2,1,0:T(8,128)S(1)}, u32[]{:S(2)}, u32[]{:S(2)}) collective-permute-start(f32[4,64,256]{2,1,0:T(8,128)S(1)} %all_gather.3), channel_id=1, source_target_pairs={{0,6},{2,0},{4,2},{6,4},{1,7},{3,1},{5,3},{7,5},{8,14},{10,8},{12,... | collective-permute-start | bytes 786440 | tf_op jit(solution)/shard_map/ppermute | solution.py:159
  143.4 1.0 copy-start.2
  174.4 1.2 copy-start.3

commit v3 on v2

v3 whole, which is shorter than its diff:
```python
import functools
import math

import jax
import jax.numpy as jnp
import ml_dtypes
import numpy as np
from jax import lax
from jax.experimental import pallas as pl
from jax.experimental.pallas import tpu as pltpu
from jax.sharding import Mesh, PartitionSpec as P

NB = 4
NR = 256
BLOCKS = 4
F32 = jnp.float32
BF16 = jnp.bfloat16


def split_table(table):
    high = table.astype(ml_dtypes.bfloat16)
    low = (table - high.astype(np.float64)).astype(ml_dtypes.bfloat16)
    return np.concatenate((high, high, low), axis=1)


def make_tables(block, scale):
    length = 2 * block
    freq = np.concatenate((np.arange(0, length, 2), np.arange(1, length, 2)))
    angle = (freq[:, None] * np.arange(block)[None, :] % length) * (2.0 * math.pi / length)
    cosine, sine = np.cos(angle), np.sin(angle)
    left = np.block([[cosine, sine], [-sine, cosine]])
    right = np.block([[cosine, -sine], [sine, cosine]])
    back = np.block([[sine.T, cosine.T], [-cosine.T, sine.T]]) * (scale / length)
    return split_table(left), split_table(right), split_table(back)


def split(values):
    high = values.astype(BF16)
    return high, (values - high.astype(F32)).astype(BF16)


def dot3(table, values):
    high, low = split(values)
    return jnp.dot(table[...], jnp.concatenate((high, low, high)), preferred_element_type=F32)


def times(a, b):
    n = a.shape[0] // 2
    ar, ai, br, bi = a[:n], a[n:], b[:n], b[n:]
    return jnp.concatenate((ar * br - ai * bi, ar * bi + ai * br))


def shifted(a):
    q = a.shape[0] // 4
    return jnp.concatenate((a[:q], -a[q : 2 * q], a[2 * q : 3 * q], -a[3 * q :]))


def pack_kernel(l_ref, g_ref, o_ref, held, read_sems, write_sems):
    groups, _, _, _, piece = o_ref.shape
    parts, _, _, _, span = held.shape
    reads = [
        pltpu.make_async_copy(
            ref.at[:, :, :, i * span : (i + 1) * span],
            held.at[i, :, 2 * side : 2 * side + 2],
            read_sems.at[2 * i + side],
        )
        for i in range(parts)
        for side, ref in enumerate((l_ref, g_ref))
    ]
    for copy in reads:
        copy.start()
    writes = []
    for i in range(parts):
        reads[2 * i].wait()
        reads[2 * i + 1].wait()
        for j in range(span // piece):
            at = i * (span // piece) + j
            source = held.at[i, :, :, :, j * piece : (j + 1) * piece]
            writes.append(pltpu.make_async_copy(source, o_ref.at[at], write_sems.at[at]))
            writes[-1].start()
    for copy in writes:
        copy.wait()


def correlate_kernel(*refs):
    stored, (x_ref, out_ref), held = refs[:3], refs[3:5], refs[5:8]
    left_ref, right_ref, back_ref = held
    x, o, read_sems, write_sems = refs[8:]
    tiles, groups, _, rows, width = x.shape
    share = groups // BLOCKS
    size = share * rows
    per = tiles // x_ref.shape[1]
    reads, writes = [], []
    for t in range(tiles):
        k, lanes = t // per, slice(t % per * width, (t % per + 1) * width)
        reads.append(pltpu.make_async_copy(x_ref.at[:, k, :, :, lanes], x.at[t], read_sems.at[t]))
        writes.append(pltpu.make_async_copy(o.at[t], out_ref.at[:, 2 * k : 2 * k + 2, :, lanes], write_sems.at[t]))
    fetches = [pltpu.make_async_copy(stored[i], held[i], read_sems.at[tiles + i]) for i in range(3)]
    for copy in (reads[0], *fetches, *reads[1:]):
        copy.start()
    for copy in fetches:
        copy.wait()
    for t in range(tiles):
        reads[t].wait()

        def pair(part, first):
            cut = slice(part * share, (part + 1) * share)
            re, im = x[t, cut, first], x[t, cut, first + 1]
            return jnp.concatenate((re.reshape(size, width), im.reshape(size, width)))

        lefts = [dot3(left_ref, pair(i, 0)) for i in range(BLOCKS)]
        rights = [dot3(right_ref, pair(i, 2)) for i in range(BLOCKS)]
        windows = rights[:1] + [shifted(rights[i - 1]) + rights[i] for i in range(1, BLOCKS)]
        for part in range(BLOCKS):
            joint = times(lefts[part], windows[0])
            for i in range(part + 1, BLOCKS):
                joint = joint + times(lefts[i], windows[i - part])
            out = dot3(back_ref, joint)
            cut = slice(part * share, (part + 1) * share)
            o[t, cut, 0] = out[:size].reshape(share, rows, width)
            o[t, cut, 1] = out[size:].reshape(share, rows, width)
        writes[t].start()
    for copy in writes:
        copy.wait()


def finish_kernel(pattern_ref, stored_ref, x_ref, pol_ref, scr_ref, xh, xl, v_ref, sems):
    groups, rows, low_energy, piece = x_ref.shape
    columns = groups * piece // (NB * NR)
    per = piece // NR
    m = rows * low_energy
    copies = [
        pltpu.make_async_copy(x_ref.at[g], pol_ref.at[:, :, g * piece : (g + 1) * piece], sems.at[g])
        for g in range(groups)
    ]
    fetch = pltpu.make_async_copy(stored_ref, v_ref, sems.at[groups])
    fetch.start()
    for copy in copies:
        copy.start()
    for c in range(columns):
        for b in range(NB):
            at = c * NB + pattern_ref[c, b]
            lane = pl.multiple_of((at % per) * NR, NR)
            high, low = split(x_ref[at // per, :, :, pl.ds(lane, NR)].reshape(m, NR))
            xh[c * m : (c + 1) * m, b * NR : (b + 1) * NR] = high
            xl[c * m : (c + 1) * m, b * NR : (b + 1) * NR] = low
    dot = functools.partial(
        lax.dot_general, dimension_numbers=(((1,), (1,)), ((), ())), preferred_element_type=F32
    )
    fetch.wait()
    total = dot(xh[...], v_ref[0]) + (dot(xl[...], v_ref[0]) + dot(xh[...], v_ref[1]))
    for c in range(columns):
        scr_ref[:, :, c * NR : (c + 1) * NR] = total[c * m : (c + 1) * m].reshape(rows, low_energy, NR)
    for copy in copies:
        copy.wait()


def partial_panels(panel_store, owner):
    me = lax.axis_index(("x", "g"))
    at = lax.axis_index("x")
    size = lax.axis_size("x")
    rows = NR // (8 * size)
    part = lax.axis_index(("y", "c"))
    mine = lax.dynamic_index_in_dim(panel_store.reshape(NB, size, 8, rows, NR), part, 2, keepdims=False)
    mine = jnp.where((owner == me)[:, None, None, None], mine, 0.0)
    total = lax.dynamic_index_in_dim(mine, at, 1, keepdims=False)
    for step in range(1, size):
        piece = lax.dynamic_index_in_dim(mine, (at + step) % size, 1, keepdims=False)
        total = total + lax.ppermute(piece, "x", [(i, (i + step) % size) for i in range(size)])
    total = total + lax.ppermute(total, "g", [(0, 1), (1, 0)])
    return lax.all_gather(total, ("y", "c"), axis=1, tiled=True)


def panels_kernel(place_ref, *refs):
    *pieces, v_ref = refs
    count = len(pieces)
    share = pieces[0].shape[1]
    for step, piece in enumerate(pieces):
        row = pl.multiple_of((place_ref[0] + count - step) % count * share, share)
        for b in range(NB):
            high, low = split(piece[b])
            v_ref[0, pl.ds(row, share), b * NR : (b + 1) * NR] = high
            v_ref[1, pl.ds(row, share), b * NR : (b + 1) * NR] = low


def whole_panels(rows):
    size = lax.axis_size("x")
    pieces = [rows]
    for step in range(1, size):
        pieces.append(lax.ppermute(rows, "x", [(i, (i + step) % size) for i in range(size)]))
    vmem = pl.BlockSpec(memory_space=pltpu.VMEM)
    return pl.pallas_call(
        panels_kernel,
        in_specs=[pl.BlockSpec(memory_space=pltpu.SMEM)] + [vmem] * size,
        out_specs=vmem,
        out_shape=jax.ShapeDtypeStruct((2, NR, NB * NR), BF16),
        compiler_params=pltpu.CompilerParams(vmem_limit_bytes=56 * 2**20),
        name="panels",
    )(lax.axis_index("x").astype(jnp.int32).reshape(1), *pieces)


def local(lesser, greater_t, panel_store, owner, pattern):
    kpoints, _, local_energy, elements = lesser.shape
    axes = ("z", "y", "c")
    groups = lax.axis_size(axes)
    total_energy = groups * local_energy
    piece = elements // groups
    tables = make_tables(total_energy // BLOCKS, 1.0 / math.sqrt(total_energy))
    panel_rows = partial_panels(panel_store, owner)
    vmem = pl.BlockSpec(memory_space=pltpu.VMEM)
    hbm = pl.BlockSpec(memory_space=pltpu.HBM)
    params = pltpu.CompilerParams(vmem_limit_bytes=24 * 2**20)

    parts = 4
    packed = pl.pallas_call(
        pack_kernel,
        in_specs=[hbm, hbm],
        out_specs=hbm,
        out_shape=jax.ShapeDtypeStruct((groups, kpoints, 4, local_energy, piece), F32),
        scratch_shapes=[
            pltpu.VMEM((parts, kpoints, 4, local_energy, elements // parts), F32),
            pltpu.SemaphoreType.DMA((2 * parts,)),
            pltpu.SemaphoreType.DMA((groups,)),
        ],
        compiler_params=pltpu.CompilerParams(vmem_limit_bytes=60 * 2**20),
        name="pack",
    )(lesser, greater_t)
    pieces = lax.all_to_all(packed, axes, 0, 0, tiled=True)
    pieces, panel_rows = lax.optimization_barrier((pieces, panel_rows))
    panels = whole_panels(panel_rows)

    rows = kpoints * 2
    width = 256
    tiles = kpoints * (piece // width)
    result = pl.pallas_call(
        correlate_kernel,
        in_specs=[hbm] * 4,
        out_specs=hbm,
        out_shape=jax.ShapeDtypeStruct((groups, rows, local_energy, piece), F32),
        scratch_shapes=[pltpu.VMEM(t.shape, BF16) for t in tables]
        + [
            pltpu.VMEM((tiles, groups, 4, local_energy, width), F32),
            pltpu.VMEM((tiles, groups, 2, local_energy, width), F32),
            pltpu.SemaphoreType.DMA((tiles + 3,)),
            pltpu.SemaphoreType.DMA((tiles,)),
        ],
        compiler_params=pltpu.CompilerParams(vmem_limit_bytes=56 * 2**20),
        name="correlate",
    )(*[jnp.asarray(t) for t in tables], pieces)
    returned = lax.all_to_all(result, axes, 0, 0, tiled=True)

    columns = elements // (NB * NR)
    polarization, screened = pl.pallas_call(
        finish_kernel,
        in_specs=[pl.BlockSpec(memory_space=pltpu.SMEM), hbm, vmem],
        out_specs=[hbm, vmem],
        out_shape=[
            jax.ShapeDtypeStruct((rows, local_energy, elements), F32),
            jax.ShapeDtypeStruct((rows, local_energy, columns * NR), F32),
        ],
        scratch_shapes=[pltpu.VMEM((columns * rows * local_energy, NB * NR), BF16)] * 2
        + [pltpu.VMEM((2, NR, NB * NR), BF16), pltpu.SemaphoreType.DMA((groups + 1,))],
        compiler_params=params,
        name="finish",
    )(pattern, panels, returned)
    return (
        polarization.reshape(kpoints, 2, local_energy, elements),
        screened.reshape(kpoints, 2, local_energy, columns * NR),
    )


def solution(mesh):
    split_mesh = Mesh(mesh.devices.reshape(4, 4, 2, 4, 2), ("z", "y", "c", "x", "g"))
    energy, matrix = ("z", "y", "c"), ("x", "g")
    in_specs = (
        P(None, None, energy, matrix),
        P(None, None, energy, matrix),
        P(matrix, None, None),
        P(),
        P(matrix, None),
    )
    out_specs = (P(None, None, energy, matrix), P(None, None, energy, matrix))
    return jax.shard_map(local, mesh=split_mesh, in_specs=in_specs, out_specs=out_specs, check_vma=False)
```

time: 181 us -> 177 us (0.978)
  local copies, waits for them, and re-layouts: 5.72 us -> 1.35 us
  waiting for transfers between devices: 110 us -> 112 us
    unnamed x19 -> x11, local copies, waits for them, and re-layouts: 3.64 us -> 1.33 us
    dynamic_update_slice x4 -> x0, local copies, waits for them, and re-layouts: 1.99 us -> none  [the longest x3 1.96 us: whole_panels(): lax.dynamic_update_slice_in_dim(panels, piece, (at - step) % size * share...]
    pallas_call x1 -> x2, Pallas kernels: 8.25 us -> 9.93 us  [the longest x1 7.62 us: local(): pl.pallas_call(correlate_kernel, in_specs=[hbm] * 4, out_specs=hbm, out_s...]
  transfers between devices with their start and end apart: 9 -> 9, of which waited for: 7 -> 8; matrix products, arithmetic and copies ran while one was open for 1% -> 0% of each run, Pallas kernels for 0% -> 1%
where the time goes in v3:
time: 177 us; the launch traced here: 176 us
  waiting for transfers between devices  112 us (63%)
  starting transfers between devices  30.5 us (17%)
  Pallas kernels  17.1 us (10%)
  blocking collectives  13.3 us (8%)
    ppermute x1, waiting for transfers between devices, partial_panels(): total = total + lax.ppermute(total, 'g', [(0, 1), (1, 0)])  61 us
    all_to_all x1, waiting for transfers between devices, local(): returned = lax.all_to_all(result, axes, 0, 0, tiled=True)  29.8 us
    all_gather x1, blocking collectives, partial_panels(): return lax.all_gather(total, ('y', 'c'), axis=1, tiled=True)  13.3 us
    ppermute x3, waiting for transfers between devices, whole_panels(): lax.ppermute(rows, 'x', [(i, (i + step) % size) for i in range(size)])  10.5 us
    all_to_all x1, starting transfers between devices, local(): pieces = lax.all_to_all(packed, axes, 0, 0, tiled=True)  9.2 us
    pallas_call x1, Pallas kernels, local(): pl.pallas_call(correlate_kernel, in_specs=[hbm] * 4, out_specs=hbm, out_s...  7.62 us
    all_to_all x1, waiting for transfers between devices, local(): pieces = lax.all_to_all(packed, axes, 0, 0, tiled=True)  6.99 us
    all_to_all x1, starting transfers between devices, local(): returned = lax.all_to_all(result, axes, 0, 0, tiled=True)  6.42 us
  transfers between devices with their start and end apart: 9, of which 8 were waited for; matrix products, arithmetic and copies ran while one was open for 0% of the time, Pallas kernels for 1%

profile of v3, /device:TPU:8, one launch (start us, length us, event | category | flops | bytes accessed | tf_op | source)
XLA Modules:
  0.0 175.5 jit_solution(14652458671966129572)
XLA Ops:
  0.6 3.8 %pack.1 = f32[32,2,4,8,512]{4,3,2,1,0:T(8,128)} custom-call(f32[2,2,8,16384]{3,2,1,0:T(8,128)} %l_ref.1, f32[2,2,8,16384]{3,2,1,0:T(8,128)} %g_ref.1), custom_call_target="tpu_custom_call" | custom-call | tf_op jit(solution)/shard_map/pack/pallas_call | solution.py:215
  4.4 9.2 %all-to-all-start = ((f32[32,2,4,8,512]{4,3,2,1,0:T(8,128)}), f32[32,2,4,8,512]{4,3,2,1,0:T(8,128)}, u32[]{:S(2)}, u32[]{:S(2)}) async-start(f32[32,2,4,8,512]{4,3,2,1,0:T(8,128)} %pack.1), calls=%async_computation | async-start | bytes 8388608 | tf_op jit(solution)/shard_map/all_to_all | solution.py:228
  13.7 0.1 bitcast_select_fusion
  13.8 2.8 %collective-permute-start.2 = (f32[4,8,256]{2,1,0:T(8,128)S(1)}, f32[4,8,256]{2,1,0:T(8,128)S(1)}, u32[]{:S(2)}, u32[]{:S(2)}) collective-permute-start(f32[4,8,256]{2,1,0:T(8,128)S(1)} %get-tuple-element.11), channel_id=1, source_target_pairs={{0,6},{2,0},{4,2},{6,4},{1,7},{3,1},{5,3},{7,5},{8,14},{10,8},{12,... | collective-permute-start | bytes 98312 | tf_op jit(solution)/shard_map/ppermute | solution.py:169
  16.7 0.8 collective-permute-start.1
  17.5 0.9 collective-permute-start
  18.3 0.1 collective-permute-done.2
  18.5 3.6 %collective-permute-done.1 = f32[4,8,256]{2,1,0:T(8,128)S(1)} collective-permute-done((f32[4,8,256]{2,1,0:T(8,128)S(1)}, f32[4,8,256]{2,1,0:T(8,128)S(1)}, u32[]{:S(2)}, u32[]{:S(2)}) %collective-permute-start.1) | collective-permute-done | bytes 32800 | tf_op jit(solution)/shard_map/ppermute | solution.py:169
  22.1 0.5 collective-permute-done
  22.6 4.6 %collective-permute-start.3 = (f32[4,8,256]{2,1,0:T(8,128)S(1)}, f32[4,8,256]{2,1,0:T(8,128)S(1)}, u32[]{:S(2)}, u32[]{:S(2)}) collective-permute-start(f32[4,8,256]{2,1,0:T(8,128)S(1)} %fusion.1), channel_id=1, source_target_pairs={{0,1},{1,0},{2,3},{3,2},{4,5},{5,4},{6,7},{7,6},{8,9},{9,8},{10,11... | collective-permute-start | bytes 98312 | tf_op jit(solution)/shard_map/ppermute | solution.py:170
  27.2 61.0 %collective-permute-done.3 = f32[4,8,256]{2,1,0:T(8,128)S(1)} collective-permute-done((f32[4,8,256]{2,1,0:T(8,128)S(1)}, f32[4,8,256]{2,1,0:T(8,128)S(1)}, u32[]{:S(2)}, u32[]{:S(2)}) %collective-permute-start.3) | collective-permute-done | bytes 32800 | tf_op jit(solution)/shard_map/ppermute | solution.py:170
  88.1 13.3 %all_gather.3.refs_0_ = f32[4,64,256]{2,1,0:T(8,128)S(1)} all-gather(f32[4,8,256]{2,1,0:T(8,128)S(1)} %add.70), channel_id=1, replica_groups=mesh['z'=4,'y'=4,'c'=2,'x'=4,'g'=2] {'y','c'}, dimensions={1}, use_global_device_ids=true | all-gather | bytes 294912 | tf_op jit(solution)/shard_map/all_gather | solution.py:171
  101.4 7.0 %all-to-all-done.refs_3_ = f32[32,2,4,8,512]{4,3,2,1,0:T(8,128)} async-done(((f32[32,2,4,8,512]{4,3,2,1,0:T(8,128)}), f32[32,2,4,8,512]{4,3,2,1,0:T(8,128)}, u32[]{:S(2)}, u32[]{:S(2)}) %all-to-all-start) | async-done | bytes 4194336 | tf_op jit(solution)/shard_map/all_to_all | solution.py:228
  108.4 7.6 %correlate.1 = f32[32,4,8,512]{3,2,1,0:T(8,128)} custom-call(bf16[256,384]{1,0:T(8,128)(2,1)} %constant.64.clone.refs_0_, bf16[256,384]{1,0:T(8,128)(2,1)} %constant.65.clone.refs_1_, bf16[128,768]{1,0:T(8,128)(2,1)} %constant.66.clone.refs_2_, f32[32,2,4,8,512]{4,3,2,1,0:T(8,128)} %all-to-all-done.refs_3_), custom_call_target="tpu_custom_call" | custom-call | tf_op jit(solution)/shard_map/correlate/pallas_call | solution.py:235
  116.1 6.4 %all-to-all-start.1 = ((f32[32,4,8,512]{3,2,1,0:T(8,128)}), f32[32,4,8,512]{3,2,1,0:T(8,128)S(1)}, u32[]{:S(2)}, u32[]{:S(2)}) async-start(f32[32,4,8,512]{3,2,1,0:T(8,128)} %correlate.1), calls=%async_computation.1 | async-start | bytes 4194304 | tf_op jit(solution)/shard_map/all_to_all | solution.py:250
  122.5 1.6 collective-permute-start.4
  124.1 2.7 %collective-permute-start.5 = (f32[4,64,256]{2,1,0:T(8,128)S(1)}, f32[4,64,256]{2,1,0:T(8,128)}, u32[]{:S(2)}, u32[]{:S(2)}) collective-permute-start(f32[4,64,256]{2,1,0:T(8,128)S(1)} %all_gather.3.refs_0_), channel_id=1, source_target_pairs={{0,4},{2,6},{4,0},{6,2},{1,5},{3,7},{5,1},{7,3},{8,12},{10,14},{12... | collective-permute-start | bytes 786440 | tf_op jit(solution)/shard_map/ppermute | solution.py:190
  126.8 1.4 collective-permute-start.6
  128.3 3.9 %collective-permute-done.4.refs_1_ = f32[4,64,256]{2,1,0:T(8,128)} collective-permute-done((f32[4,64,256]{2,1,0:T(8,128)S(1)}, f32[4,64,256]{2,1,0:T(8,128)}, u32[]{:S(2)}, u32[]{:S(2)}) %collective-permute-start.4) | collective-permute-done | bytes 262176 | tf_op jit(solution)/shard_map/ppermute | solution.py:190
  132.2 6.6 %collective-permute-done.5.refs_2_ = f32[4,64,256]{2,1,0:T(8,128)} collective-permute-done((f32[4,64,256]{2,1,0:T(8,128)S(1)}, f32[4,64,256]{2,1,0:T(8,128)}, u32[]{:S(2)}, u32[]{:S(2)}) %collective-permute-start.5) | collective-permute-done | bytes 262176 | tf_op jit(solution)/shard_map/ppermute | solution.py:190
  138.8 2.3 %panels.1.stored_ref = bf16[2,256,1024]{2,1,0:T(8,128)(2,1)} custom-call(s32[1]{0:T(128)} %bitcast.place_ref, f32[4,64,256]{2,1,0:T(8,128)} %copy-done.2, f32[4,64,256]{2,1,0:T(8,128)} %collective-permute-done.4.refs_1_, f32[4,64,256]{2,1,0:T(8,128)} %collective-permute-done.5.refs_2_, f32[4,64,256]{2,1,0:T(8,128)} %collective-permute-done.6.refs_3_), custom_call_target="tpu_custom_call" | custom-call | tf_op jit(solution)/shard_map/panels/pallas_call | solution.py:192
  141.2 29.8 %all-to-all-done.1.x_ref = f32[32,4,8,512]{3,2,1,0:T(8,128)S(1)} async-done(((f32[32,4,8,512]{3,2,1,0:T(8,128)}), f32[32,4,8,512]{3,2,1,0:T(8,128)S(1)}, u32[]{:S(2)}, u32[]{:S(2)}) %all-to-all-start.1) | async-done | bytes 2097184 | tf_op jit(solution)/shard_map/all_to_all | solution.py:250
  170.9 1.2 copy-done.1
  172.1 3.4 %finish.1 = (f32[4,8,16384]{2,1,0:T(8,128)}, f32[4,8,4096]{2,1,0:T(8,128)}) custom-call(s32[16,4]{1,0:T(8,128)S(1)} %copy.11.pattern_ref, bf16[2,256,1024]{2,1,0:T(8,128)(2,1)S(1)} %copy-done.1, f32[32,4,8,512]{3,2,1,0:T(8,128)S(1)} %all-to-all-done.1.x_ref), custom_call_target="tpu_custom_call" | custom-call | tf_op jit(solution)/shard_map/finish/pallas_call | solution.py:253
  (15 shorter events, 0.2 us)
Async XLA Ops:
  0.6 13.1 %copy-start = (f32[4,256,256]{2,1,0:T(8,128)S(1)}, f32[4,256,256]{2,1,0:T(8,128)}, u32[]{:S(2)}) copy-start(f32[4,256,256]{2,1,0:T(8,128)} %param.10) | copy-start | bytes 3145732
  4.4 9.3 %copy-start.4 = (s32[4]{0:T(128)S(1)}, s32[4]{0:T(128)}, u32[]{:S(2)}) copy-start(s32[4]{0:T(128)} %param.11) | copy-start | bytes 52
  4.4 104.0 %all-to-all-start = ((f32[32,2,4,8,512]{4,3,2,1,0:T(8,128)}), f32[32,2,4,8,512]{4,3,2,1,0:T(8,128)}, u32[]{:S(2)}, u32[]{:S(2)}) async-start(f32[32,2,4,8,512]{4,3,2,1,0:T(8,128)} %pack.1), calls=%async_computation | async-start | bytes 8388608 | tf_op jit(solution)/shard_map/all_to_all | solution.py:228
  13.8 4.7 %collective-permute-start.2 = (f32[4,8,256]{2,1,0:T(8,128)S(1)}, f32[4,8,256]{2,1,0:T(8,128)S(1)}, u32[]{:S(2)}, u32[]{:S(2)}) collective-permute-start(f32[4,8,256]{2,1,0:T(8,128)S(1)} %get-tuple-element.11), channel_id=1, source_target_pairs={{0,6},{2,0},{4,2},{6,4},{1,7},{3,1},{5,3},{7,5},{8,14},{10,8},{12,... | collective-permute-start | bytes 98312 | tf_op jit(solution)/shard_map/ppermute | solution.py:169
  16.7 5.4 %collective-permute-start.1 = (f32[4,8,256]{2,1,0:T(8,128)S(1)}, f32[4,8,256]{2,1,0:T(8,128)S(1)}, u32[]{:S(2)}, u32[]{:S(2)}) collective-permute-start(f32[4,8,256]{2,1,0:T(8,128)S(1)} %get-tuple-element.12), channel_id=1, source_target_pairs={{0,4},{2,6},{4,0},{6,2},{1,5},{3,7},{5,1},{7,3},{8,12},{10,14},{12... | collective-permute-start | bytes 98312 | tf_op jit(solution)/shard_map/ppermute | solution.py:169
  17.5 5.1 %collective-permute-start = (f32[4,8,256]{2,1,0:T(8,128)S(1)}, f32[4,8,256]{2,1,0:T(8,128)S(1)}, u32[]{:S(2)}, u32[]{:S(2)}) collective-permute-start(f32[4,8,256]{2,1,0:T(8,128)S(1)} %get-tuple-element.10), channel_id=1, source_target_pairs={{0,2},{2,4},{4,6},{6,0},{1,3},{3,5},{5,7},{7,1},{8,10},{10,12},{12... | collective-permute-start | bytes 98312 | tf_op jit(solution)/shard_map/ppermute | solution.py:169
  22.6 65.5 %collective-permute-start.3 = (f32[4,8,256]{2,1,0:T(8,128)S(1)}, f32[4,8,256]{2,1,0:T(8,128)S(1)}, u32[]{:S(2)}, u32[]{:S(2)}) collective-permute-start(f32[4,8,256]{2,1,0:T(8,128)S(1)} %fusion.1), channel_id=1, source_target_pairs={{0,1},{1,0},{2,3},{3,2},{4,5},{5,4},{6,7},{7,6},{8,9},{9,8},{10,11... | collective-permute-start | bytes 98312 | tf_op jit(solution)/shard_map/ppermute | solution.py:170
  101.4 25.4 %copy-start.2 = (f32[4,64,256]{2,1,0:T(8,128)}, f32[4,64,256]{2,1,0:T(8,128)S(1)}, u32[]{:S(2)}) copy-start(f32[4,64,256]{2,1,0:T(8,128)S(1)} %all_gather.3.refs_0_) | copy-start | bytes 786436
  116.1 12.2 %copy-start.3 = (s32[16,4]{0,1:T(4,128)S(1)}, s32[16,4]{0,1:T(4,128)}, u32[]{:S(2)}) copy-start(s32[16,4]{0,1:T(4,128)} %param.12) | copy-start | bytes 772
  116.1 54.8 %all-to-all-start.1 = ((f32[32,4,8,512]{3,2,1,0:T(8,128)}), f32[32,4,8,512]{3,2,1,0:T(8,128)S(1)}, u32[]{:S(2)}, u32[]{:S(2)}) async-start(f32[32,4,8,512]{3,2,1,0:T(8,128)} %correlate.1), calls=%async_computation.1 | async-start | bytes 4194304 | tf_op jit(solution)/shard_map/all_to_all | solution.py:250
  122.5 9.8 %collective-permute-start.4 = (f32[4,64,256]{2,1,0:T(8,128)S(1)}, f32[4,64,256]{2,1,0:T(8,128)}, u32[]{:S(2)}, u32[]{:S(2)}) collective-permute-start(f32[4,64,256]{2,1,0:T(8,128)S(1)} %all_gather.3.refs_0_), channel_id=1, source_target_pairs={{0,2},{2,4},{4,6},{6,0},{1,3},{3,5},{5,7},{7,1},{8,10},{10,12},{12... | collective-permute-start | bytes 786440 | tf_op jit(solution)/shard_map/ppermute | solution.py:190
  124.1 14.8 %collective-permute-start.5 = (f32[4,64,256]{2,1,0:T(8,128)S(1)}, f32[4,64,256]{2,1,0:T(8,128)}, u32[]{:S(2)}, u32[]{:S(2)}) collective-permute-start(f32[4,64,256]{2,1,0:T(8,128)S(1)} %all_gather.3.refs_0_), channel_id=1, source_target_pairs={{0,4},{2,6},{4,0},{6,2},{1,5},{3,7},{5,1},{7,3},{8,12},{10,14},{12... | collective-permute-start | bytes 786440 | tf_op jit(solution)/shard_map/ppermute | solution.py:190
  126.8 12.1 %collective-permute-start.6 = (f32[4,64,256]{2,1,0:T(8,128)S(1)}, f32[4,64,256]{2,1,0:T(8,128)}, u32[]{:S(2)}, u32[]{:S(2)}) collective-permute-start(f32[4,64,256]{2,1,0:T(8,128)S(1)} %all_gather.3.refs_0_), channel_id=1, source_target_pairs={{0,6},{2,0},{4,2},{6,4},{1,7},{3,1},{5,3},{7,5},{8,14},{10,8},{12,... | collective-permute-start | bytes 786440 | tf_op jit(solution)/shard_map/ppermute | solution.py:190
  170.9 1.2 copy-start.1

commit v4 on v3

--- a/solution.py
+++ b/solution.py
@@ -86,15 +86,14 @@
     stored, (x_ref, out_ref), held = refs[:3], refs[3:5], refs[5:8]
     left_ref, right_ref, back_ref = held
     x, o, read_sems, write_sems = refs[8:]
-    tiles, groups, _, rows, width = x.shape
-    share = groups // BLOCKS
+    tiles, share, _, _, rows, width = x.shape
     size = share * rows
-    per = tiles // x_ref.shape[1]
+    per = tiles // x_ref.shape[2]
     reads, writes = [], []
     for t in range(tiles):
         k, lanes = t // per, slice(t % per * width, (t % per + 1) * width)
-        reads.append(pltpu.make_async_copy(x_ref.at[:, k, :, :, lanes], x.at[t], read_sems.at[t]))
-        writes.append(pltpu.make_async_copy(o.at[t], out_ref.at[:, 2 * k : 2 * k + 2, :, lanes], write_sems.at[t]))
+        reads.append(pltpu.make_async_copy(x_ref.at[:, :, k, :, :, lanes], x.at[t], read_sems.at[t]))
+        writes.append(pltpu.make_async_copy(o.at[t], out_ref.at[:, :, 2 * k : 2 * k + 2, :, lanes], write_sems.at[t]))
     fetches = [pltpu.make_async_copy(stored[i], held[i], read_sems.at[tiles + i]) for i in range(3)]
     for copy in (reads[0], *fetches, *reads[1:]):
         copy.start()
@@ -104,8 +103,7 @@
         reads[t].wait()
 
         def pair(part, first):
-            cut = slice(part * share, (part + 1) * share)
-            re, im = x[t, cut, first], x[t, cut, first + 1]
+            re, im = x[t, :, part, first], x[t, :, part, first + 1]
             return jnp.concatenate((re.reshape(size, width), im.reshape(size, width)))
 
         lefts = [dot3(left_ref, pair(i, 0)) for i in range(BLOCKS)]
@@ -116,9 +114,8 @@
             for i in range(part + 1, BLOCKS):
                 joint = joint + times(lefts[i], windows[i - part])
             out = dot3(back_ref, joint)
-            cut = slice(part * share, (part + 1) * share)
-            o[t, cut, 0] = out[:size].reshape(share, rows, width)
-            o[t, cut, 1] = out[size:].reshape(share, rows, width)
+            o[t, :, part, 0] = out[:size].reshape(share, rows, width)
+            o[t, :, part, 1] = out[size:].reshape(share, rows, width)
         writes[t].start()
     for copy in writes:
         copy.wait()
@@ -137,20 +134,33 @@
     fetch.start()
     for copy in copies:
         copy.start()
-    for c in range(columns):
-        for b in range(NB):
-            at = c * NB + pattern_ref[c, b]
-            lane = pl.multiple_of((at % per) * NR, NR)
-            high, low = split(x_ref[at // per, :, :, pl.ds(lane, NR)].reshape(m, NR))
-            xh[c * m : (c + 1) * m, b * NR : (b + 1) * NR] = high
-            xl[c * m : (c + 1) * m, b * NR : (b + 1) * NR] = low
     dot = functools.partial(
         lax.dot_general, dimension_numbers=(((1,), (1,)), ((), ())), preferred_element_type=F32
     )
+
+    def gather(first, last):
+        for c in range(first, last):
+            for b in range(NB):
+                at = c * NB + pattern_ref[c, b]
+                lane = pl.multiple_of((at % per) * NR, NR)
+                high, low = split(x_ref[at // per, :, :, pl.ds(lane, NR)].reshape(m, NR))
+                xh[c * m : (c + 1) * m, b * NR : (b + 1) * NR] = high
+                xl[c * m : (c + 1) * m, b * NR : (b + 1) * NR] = low
+
+    def product(first, last):
+        cut = slice(first * m, last * m)
+        total = dot(xh[cut], v_ref[0]) + (dot(xl[cut], v_ref[0]) + dot(xh[cut], v_ref[1]))
+        for c in range(first, last):
+            row = (c - first) * m
+            scr_ref[:, :, c * NR : (c + 1) * NR] = total[row : row + m].reshape(rows, low_energy, NR)
+
+    group = columns // 2
+    gather(0, group)
     fetch.wait()
-    total = dot(xh[...], v_ref[0]) + (dot(xl[...], v_ref[0]) + dot(xh[...], v_ref[1]))
-    for c in range(columns):
-        scr_ref[:, :, c * NR : (c + 1) * NR] = total[c * m : (c + 1) * m].reshape(rows, low_energy, NR)
+    for first in range(0, columns, group):
+        if first + group < columns:
+            gather(first + group, first + 2 * group)
+        product(first, first + group)
     for copy in copies:
         copy.wait()
 
@@ -201,7 +211,7 @@
 
 def local(lesser, greater_t, panel_store, owner, pattern):
     kpoints, _, local_energy, elements = lesser.shape
-    axes = ("z", "y", "c")
+    axes = ("y", "c", "z")
     groups = lax.axis_size(axes)
     total_energy = groups * local_energy
     piece = elements // groups
@@ -236,18 +246,18 @@
         correlate_kernel,
         in_specs=[hbm] * 4,
         out_specs=hbm,
-        out_shape=jax.ShapeDtypeStruct((groups, rows, local_energy, piece), F32),
+        out_shape=jax.ShapeDtypeStruct((groups // BLOCKS, BLOCKS, rows, local_energy, piece), F32),
         scratch_shapes=[pltpu.VMEM(t.shape, BF16) for t in tables]
         + [
-            pltpu.VMEM((tiles, groups, 4, local_energy, width), F32),
-            pltpu.VMEM((tiles, groups, 2, local_energy, width), F32),
+            pltpu.VMEM((tiles, groups // BLOCKS, BLOCKS, 4, local_energy, width), F32),
+            pltpu.VMEM((tiles, groups // BLOCKS, BLOCKS, 2, local_energy, width), F32),
             pltpu.SemaphoreType.DMA((tiles + 3,)),
             pltpu.SemaphoreType.DMA((tiles,)),
         ],
         compiler_params=pltpu.CompilerParams(vmem_limit_bytes=56 * 2**20),
         name="correlate",
-    )(*[jnp.asarray(t) for t in tables], pieces)
-    returned = lax.all_to_all(result, axes, 0, 0, tiled=True)
+    )(*[jnp.asarray(t) for t in tables], pieces.reshape(groups // BLOCKS, BLOCKS, kpoints, 4, local_energy, piece))
+    returned = lax.all_to_all(result.reshape(groups, rows, local_energy, piece), axes, 0, 0, tiled=True)
 
     columns = elements // (NB * NR)
     polarization, screened = pl.pallas_call(

time: 177 us -> 176 us (level); the launches traced: 176 us -> 172 us
  waiting for transfers between devices: 112 us -> 106 us
  starting transfers between devices: 30.5 us -> 32.6 us
    all_to_all x1, waiting for transfers between devices: 6.99 us -> 0.73 us  [local(): pieces = lax.all_to_all(packed, axes, 0, 0, tiled=True)]
    all_to_all x1, starting transfers between devices: 6.42 us -> 8.57 us  [local(): lax.all_to_all(result.reshape(groups, rows, local_energy, piece), axes, 0...]
    ppermute x1, waiting for transfers between devices: 61 us -> 63.1 us  [partial_panels(): total = total + lax.ppermute(total, 'g', [(0, 1), (1, 0)])]
    all_to_all x1, waiting for transfers between devices: 29.8 us -> 27.9 us  [local(): lax.all_to_all(result.reshape(groups, rows, local_energy, piece), axes, 0...]
where the time goes in v4:
time: 176 us; the launch traced here: 172 us
  waiting for transfers between devices  106 us (60%)
  starting transfers between devices  32.6 us (19%)
  Pallas kernels  16.9 us (10%)
  blocking collectives  14.3 us (8%)
    ppermute x1, waiting for transfers between devices, partial_panels(): total = total + lax.ppermute(total, 'g', [(0, 1), (1, 0)])  63.1 us
    all_to_all x1, waiting for transfers between devices, local(): lax.all_to_all(result.reshape(groups, rows, local_energy, piece), axes, 0...  27.9 us
    all_gather x1, blocking collectives, partial_panels(): return lax.all_gather(total, ('y', 'c'), axis=1, tiled=True)  14.3 us
    ppermute x3, waiting for transfers between devices, whole_panels(): lax.ppermute(rows, 'x', [(i, (i + step) % size) for i in range(size)])  10.5 us
    all_to_all x1, starting transfers between devices, local(): pieces = lax.all_to_all(packed, axes, 0, 0, tiled=True)  9.21 us
    all_to_all x1, starting transfers between devices, local(): lax.all_to_all(result.reshape(groups, rows, local_energy, piece), axes, 0...  8.57 us
    pallas_call x1, Pallas kernels, local(): pl.pallas_call(correlate_kernel, in_specs=[hbm] * 4, out_specs=hbm, out_s...  7.62 us
    ppermute x3, starting transfers between devices, whole_panels(): lax.ppermute(rows, 'x', [(i, (i + step) % size) for i in range(size)])  5.74 us
  transfers between devices with their start and end apart: 9, of which 8 were waited for; matrix products, arithmetic and copies ran while one was open for 0% of the time, Pallas kernels for 1%

profile of v4, /device:TPU:8, one launch (start us, length us, event | category | flops | bytes accessed | tf_op | source)
XLA Modules:
  0.0 172.4 jit_solution(7430177480586587702)
XLA Ops:
  0.6 3.8 %pack.1 = f32[32,2,4,8,512]{4,3,2,1,0:T(8,128)} custom-call(f32[2,2,8,16384]{3,2,1,0:T(8,128)} %l_ref.1, f32[2,2,8,16384]{3,2,1,0:T(8,128)} %g_ref.1), custom_call_target="tpu_custom_call" | custom-call | tf_op jit(solution)/shard_map/pack/pallas_call | solution.py:225
  4.4 9.2 %all-to-all-start = ((f32[32,2,4,8,512]{4,3,2,1,0:T(8,128)}), f32[32,2,4,8,512]{4,3,2,1,0:T(8,128)}, u32[]{:S(2)}, u32[]{:S(2)}) async-start(f32[32,2,4,8,512]{4,3,2,1,0:T(8,128)} %pack.1), calls=%async_computation | async-start | bytes 8388608 | tf_op jit(solution)/shard_map/all_to_all | solution.py:238
  13.7 0.1 bitcast_select_fusion
  13.8 2.8 %collective-permute-start.2 = (f32[4,8,256]{2,1,0:T(8,128)S(1)}, f32[4,8,256]{2,1,0:T(8,128)S(1)}, u32[]{:S(2)}, u32[]{:S(2)}) collective-permute-start(f32[4,8,256]{2,1,0:T(8,128)S(1)} %get-tuple-element.11), channel_id=1, source_target_pairs={{0,6},{2,0},{4,2},{6,4},{1,7},{3,1},{5,3},{7,5},{8,14},{10,8},{12,... | collective-permute-start | bytes 98312 | tf_op jit(solution)/shard_map/ppermute | solution.py:179
  16.7 0.8 collective-permute-start.1
  17.5 0.9 collective-permute-start
  18.3 0.1 collective-permute-done.2
  18.5 3.6 %collective-permute-done.1 = f32[4,8,256]{2,1,0:T(8,128)S(1)} collective-permute-done((f32[4,8,256]{2,1,0:T(8,128)S(1)}, f32[4,8,256]{2,1,0:T(8,128)S(1)}, u32[]{:S(2)}, u32[]{:S(2)}) %collective-permute-start.1) | collective-permute-done | bytes 32800 | tf_op jit(solution)/shard_map/ppermute | solution.py:179
  22.1 0.5 collective-permute-done
  22.6 4.6 %collective-permute-start.3 = (f32[4,8,256]{2,1,0:T(8,128)S(1)}, f32[4,8,256]{2,1,0:T(8,128)S(1)}, u32[]{:S(2)}, u32[]{:S(2)}) collective-permute-start(f32[4,8,256]{2,1,0:T(8,128)S(1)} %fusion.1), channel_id=1, source_target_pairs={{0,1},{1,0},{2,3},{3,2},{4,5},{5,4},{6,7},{7,6},{8,9},{9,8},{10,11... | collective-permute-start | bytes 98312 | tf_op jit(solution)/shard_map/ppermute | solution.py:180
  27.2 63.1 %collective-permute-done.3 = f32[4,8,256]{2,1,0:T(8,128)S(1)} collective-permute-done((f32[4,8,256]{2,1,0:T(8,128)S(1)}, f32[4,8,256]{2,1,0:T(8,128)S(1)}, u32[]{:S(2)}, u32[]{:S(2)}) %collective-permute-start.3) | collective-permute-done | bytes 32800 | tf_op jit(solution)/shard_map/ppermute | solution.py:180
  90.3 14.3 %all_gather.3.refs_0_ = f32[4,64,256]{2,1,0:T(8,128)S(1)} all-gather(f32[4,8,256]{2,1,0:T(8,128)S(1)} %add.70), channel_id=1, replica_groups=mesh['z'=4,'y'=4,'c'=2,'x'=4,'g'=2] {'y','c'}, dimensions={1}, use_global_device_ids=true | all-gather | bytes 294912 | tf_op jit(solution)/shard_map/all_gather | solution.py:181
  104.5 0.7 all-to-all-done
  105.3 7.6 %correlate.1 = f32[8,4,4,8,512]{4,3,2,1,0:T(8,128)} custom-call(bf16[256,384]{1,0:T(8,128)(2,1)} %constant.64.clone.refs_0_, bf16[256,384]{1,0:T(8,128)(2,1)} %constant.65.clone.refs_1_, bf16[128,768]{1,0:T(8,128)(2,1)} %constant.66.clone.refs_2_, f32[8,4,2,4,8,512]{5,4,3,2,1,0:T(8,128)} %bitcast.7.refs_3_), custom_call_target="tpu_custom_call" | custom-call | tf_op jit(solution)/shard_map/correlate/pallas_call | solution.py:245
  112.9 8.6 %all-to-all-start.1 = ((f32[32,4,8,512]{3,2,1,0:T(8,128)}), f32[32,4,8,512]{3,2,1,0:T(8,128)S(1)}, u32[]{:S(2)}, u32[]{:S(2)}) async-start(f32[32,4,8,512]{3,2,1,0:T(8,128)} %bitcast.21), calls=%async_computation.1 | async-start | bytes 4194304 | tf_op jit(solution)/shard_map/all_to_all | solution.py:260
  121.5 1.6 collective-permute-start.4
  123.1 2.7 %collective-permute-start.5 = (f32[4,64,256]{2,1,0:T(8,128)S(1)}, f32[4,64,256]{2,1,0:T(8,128)}, u32[]{:S(2)}, u32[]{:S(2)}) collective-permute-start(f32[4,64,256]{2,1,0:T(8,128)S(1)} %all_gather.3.refs_0_), channel_id=1, source_target_pairs={{0,4},{2,6},{4,0},{6,2},{1,5},{3,7},{5,1},{7,3},{8,12},{10,14},{12... | collective-permute-start | bytes 786440 | tf_op jit(solution)/shard_map/ppermute | solution.py:200
  125.8 1.4 collective-permute-start.6
  127.3 3.9 %collective-permute-done.4.refs_1_ = f32[4,64,256]{2,1,0:T(8,128)} collective-permute-done((f32[4,64,256]{2,1,0:T(8,128)S(1)}, f32[4,64,256]{2,1,0:T(8,128)}, u32[]{:S(2)}, u32[]{:S(2)}) %collective-permute-start.4) | collective-permute-done | bytes 262176 | tf_op jit(solution)/shard_map/ppermute | solution.py:200
  131.2 6.6 %collective-permute-done.5.refs_2_ = f32[4,64,256]{2,1,0:T(8,128)} collective-permute-done((f32[4,64,256]{2,1,0:T(8,128)S(1)}, f32[4,64,256]{2,1,0:T(8,128)}, u32[]{:S(2)}, u32[]{:S(2)}) %collective-permute-start.5) | collective-permute-done | bytes 262176 | tf_op jit(solution)/shard_map/ppermute | solution.py:200
  137.9 2.3 %panels.1.stored_ref = bf16[2,256,1024]{2,1,0:T(8,128)(2,1)} custom-call(s32[1]{0:T(128)} %bitcast.place_ref, f32[4,64,256]{2,1,0:T(8,128)} %copy-done.2, f32[4,64,256]{2,1,0:T(8,128)} %collective-permute-done.4.refs_1_, f32[4,64,256]{2,1,0:T(8,128)} %collective-permute-done.5.refs_2_, f32[4,64,256]{2,1,0:T(8,128)} %collective-permute-done.6.refs_3_), custom_call_target="tpu_custom_call" | custom-call | tf_op jit(solution)/shard_map/panels/pallas_call | solution.py:202
  140.2 27.9 %all-to-all-done.1.x_ref = f32[32,4,8,512]{3,2,1,0:T(8,128)S(1)} async-done(((f32[32,4,8,512]{3,2,1,0:T(8,128)}), f32[32,4,8,512]{3,2,1,0:T(8,128)S(1)}, u32[]{:S(2)}, u32[]{:S(2)}) %all-to-all-start.1) | async-done | bytes 2097184 | tf_op jit(solution)/shard_map/all_to_all | solution.py:260
  168.0 1.2 copy-done.1
  169.2 3.2 %finish.1 = (f32[4,8,16384]{2,1,0:T(8,128)}, f32[4,8,4096]{2,1,0:T(8,128)}) custom-call(s32[16,4]{1,0:T(8,128)S(1)} %copy.11.pattern_ref, bf16[2,256,1024]{2,1,0:T(8,128)(2,1)S(1)} %copy-done.1, f32[32,4,8,512]{3,2,1,0:T(8,128)S(1)} %all-to-all-done.1.x_ref), custom_call_target="tpu_custom_call" | custom-call | tf_op jit(solution)/shard_map/finish/pallas_call | solution.py:263
  (15 shorter events, 0.2 us)
Async XLA Ops:
  0.6 13.1 %copy-start = (f32[4,256,256]{2,1,0:T(8,128)S(1)}, f32[4,256,256]{2,1,0:T(8,128)}, u32[]{:S(2)}) copy-start(f32[4,256,256]{2,1,0:T(8,128)} %param.10) | copy-start | bytes 3145732
  4.4 9.3 %copy-start.4 = (s32[4]{0:T(128)S(1)}, s32[4]{0:T(128)}, u32[]{:S(2)}) copy-start(s32[4]{0:T(128)} %param.11) | copy-start | bytes 52
  4.4 100.9 %all-to-all-start = ((f32[32,2,4,8,512]{4,3,2,1,0:T(8,128)}), f32[32,2,4,8,512]{4,3,2,1,0:T(8,128)}, u32[]{:S(2)}, u32[]{:S(2)}) async-start(f32[32,2,4,8,512]{4,3,2,1,0:T(8,128)} %pack.1), calls=%async_computation | async-start | bytes 8388608 | tf_op jit(solution)/shard_map/all_to_all | solution.py:238
  13.8 4.7 %collective-permute-start.2 = (f32[4,8,256]{2,1,0:T(8,128)S(1)}, f32[4,8,256]{2,1,0:T(8,128)S(1)}, u32[]{:S(2)}, u32[]{:S(2)}) collective-permute-start(f32[4,8,256]{2,1,0:T(8,128)S(1)} %get-tuple-element.11), channel_id=1, source_target_pairs={{0,6},{2,0},{4,2},{6,4},{1,7},{3,1},{5,3},{7,5},{8,14},{10,8},{12,... | collective-permute-start | bytes 98312 | tf_op jit(solution)/shard_map/ppermute | solution.py:179
  16.7 5.4 %collective-permute-start.1 = (f32[4,8,256]{2,1,0:T(8,128)S(1)}, f32[4,8,256]{2,1,0:T(8,128)S(1)}, u32[]{:S(2)}, u32[]{:S(2)}) collective-permute-start(f32[4,8,256]{2,1,0:T(8,128)S(1)} %get-tuple-element.12), channel_id=1, source_target_pairs={{0,4},{2,6},{4,0},{6,2},{1,5},{3,7},{5,1},{7,3},{8,12},{10,14},{12... | collective-permute-start | bytes 98312 | tf_op jit(solution)/shard_map/ppermute | solution.py:179
  17.5 5.1 %collective-permute-start = (f32[4,8,256]{2,1,0:T(8,128)S(1)}, f32[4,8,256]{2,1,0:T(8,128)S(1)}, u32[]{:S(2)}, u32[]{:S(2)}) collective-permute-start(f32[4,8,256]{2,1,0:T(8,128)S(1)} %get-tuple-element.10), channel_id=1, source_target_pairs={{0,2},{2,4},{4,6},{6,0},{1,3},{3,5},{5,7},{7,1},{8,10},{10,12},{12... | collective-permute-start | bytes 98312 | tf_op jit(solution)/shard_map/ppermute | solution.py:179
  22.6 67.7 %collective-permute-start.3 = (f32[4,8,256]{2,1,0:T(8,128)S(1)}, f32[4,8,256]{2,1,0:T(8,128)S(1)}, u32[]{:S(2)}, u32[]{:S(2)}) collective-permute-start(f32[4,8,256]{2,1,0:T(8,128)S(1)} %fusion.1), channel_id=1, source_target_pairs={{0,1},{1,0},{2,3},{3,2},{4,5},{5,4},{6,7},{7,6},{8,9},{9,8},{10,11... | collective-permute-start | bytes 98312 | tf_op jit(solution)/shard_map/ppermute | solution.py:180
  104.5 21.3 %copy-start.2 = (f32[4,64,256]{2,1,0:T(8,128)}, f32[4,64,256]{2,1,0:T(8,128)S(1)}, u32[]{:S(2)}) copy-start(f32[4,64,256]{2,1,0:T(8,128)S(1)} %all_gather.3.refs_0_) | copy-start | bytes 786436
  112.9 14.3 %copy-start.3 = (s32[16,4]{0,1:T(4,128)S(1)}, s32[16,4]{0,1:T(4,128)}, u32[]{:S(2)}) copy-start(s32[16,4]{0,1:T(4,128)} %param.12) | copy-start | bytes 772
  112.9 55.1 %all-to-all-start.1 = ((f32[32,4,8,512]{3,2,1,0:T(8,128)}), f32[32,4,8,512]{3,2,1,0:T(8,128)S(1)}, u32[]{:S(2)}, u32[]{:S(2)}) async-start(f32[32,4,8,512]{3,2,1,0:T(8,128)} %bitcast.21), calls=%async_computation.1 | async-start | bytes 4194304 | tf_op jit(solution)/shard_map/all_to_all | solution.py:260
  121.5 9.8 %collective-permute-start.4 = (f32[4,64,256]{2,1,0:T(8,128)S(1)}, f32[4,64,256]{2,1,0:T(8,128)}, u32[]{:S(2)}, u32[]{:S(2)}) collective-permute-start(f32[4,64,256]{2,1,0:T(8,128)S(1)} %all_gather.3.refs_0_), channel_id=1, source_target_pairs={{0,2},{2,4},{4,6},{6,0},{1,3},{3,5},{5,7},{7,1},{8,10},{10,12},{12... | collective-permute-start | bytes 786440 | tf_op jit(solution)/shard_map/ppermute | solution.py:200
  123.1 14.8 %collective-permute-start.5 = (f32[4,64,256]{2,1,0:T(8,128)S(1)}, f32[4,64,256]{2,1,0:T(8,128)}, u32[]{:S(2)}, u32[]{:S(2)}) collective-permute-start(f32[4,64,256]{2,1,0:T(8,128)S(1)} %all_gather.3.refs_0_), channel_id=1, source_target_pairs={{0,4},{2,6},{4,0},{6,2},{1,5},{3,7},{5,1},{7,3},{8,12},{10,14},{12... | collective-permute-start | bytes 786440 | tf_op jit(solution)/shard_map/ppermute | solution.py:200
  125.8 12.1 %collective-permute-start.6 = (f32[4,64,256]{2,1,0:T(8,128)S(1)}, f32[4,64,256]{2,1,0:T(8,128)}, u32[]{:S(2)}, u32[]{:S(2)}) collective-permute-start(f32[4,64,256]{2,1,0:T(8,128)S(1)} %all_gather.3.refs_0_), channel_id=1, source_target_pairs={{0,6},{2,0},{4,2},{6,4},{1,7},{3,1},{5,3},{7,5},{8,14},{10,8},{12,... | collective-permute-start | bytes 786440 | tf_op jit(solution)/shard_map/ppermute | solution.py:200
  168.0 1.2 copy-start.1
